TPU v7x, 32 devices: a whole 2x2x4 slice. The times are simulated.
32 devices in a mesh: pipe: 2 (over x), dp: 4 (over y, core), tensor: 4 (over z).
Axes of the slice: x: 2, y: 2, z: 4, core: 2. Of those that a mesh axis runs over, the one named last changes fastest.
Arguments:
- section_rows: bfloat16 [2, 8, 2, 256, 768], P('pipe', 'dp', None, 'tensor'), may hold values from -6 to 6
- enc_lengths: int32 [8, 6], P('dp'), may hold values from 1 to 256, 512 in all within a row
- dec_lengths: int32 [8, 6], P('dp'), may hold values from 1 to 114, 256 in all within a row
- enc_buckets: int32 [1023], replicated, may hold values from 0 to 31
- dec_buckets: int32 [256], replicated, may hold values from 0 to 31
- norm_gains: float32 [2, 3, 768], P('pipe'), may hold values from 0.5 to 1.5
- rel_bias: float32 [2, 32, 12], P('pipe', None, 'tensor'), may hold values from -3 to 3
- query_key_w: bfloat16 [2, 2, 768, 768], P('pipe', None, 'dp', 'tensor'), may hold values from -0.078125 to 0.078125
- value_w: bfloat16 [2, 768, 768], P('pipe', 'dp', 'tensor'), may hold values from -0.21875 to 0.21875
- attn_out_w: bfloat16 [2, 768, 768], P('pipe', 'tensor', 'dp'), may hold values from -1 to 1
- cross_first: bfloat16 [2, 768, 768], P('pipe', 'dp', 'tensor'), may hold values from -0.078125 to 0.078125
- cross_second: bfloat16 [2, 768, 768], P('pipe', 'dp', 'tensor'), may hold values from -0.5 to 0.5
- ff_in: bfloat16 [2, 768, 3072], P('pipe', 'dp', 'tensor'), may hold values from -0.21875 to 0.21875
- ff_out: bfloat16 [2, 3072, 768], P('pipe', 'tensor', 'dp'), may hold values from -0.109375 to 0.109375
Outputs:
- section_out: float32 [2, 8, 2, 256, 768], P('pipe', 'dp', None, 'tensor')
- gain_grads: float32 [2, 3, 768], P('pipe', None, 'dp')
- bias_grads: float32 [2, 32, 12], P('pipe', 'dp', 'tensor')
- pair_grads: float32 [2, 2, 768, 768], P('pipe', None, 'dp', 'tensor')
- value_grads: float32 [2, 768, 768], P('pipe', 'dp', 'tensor')
- out_grads: float32 [2, 768, 768], P('pipe', 'tensor', 'dp')
- first_grads: float32 [2, 768, 768], P('pipe', 'dp', 'tensor')
- second_grads: float32 [2, 768, 768], P('pipe', 'dp', 'tensor')
- inner_grads: float32 [2, 768, 3072], P('pipe', 'dp', 'tensor')
- outer_grads: float32 [2, 3072, 768], P('pipe', 'tensor', 'dp')
Inputs may be any that keep to these rules, and one draw needn't show every extreme that they name: `enc_lengths`: each row's 6 lengths sum to 512; one of them is exactly 256. `dec_lengths`: each row's 6 lengths sum to 256; one of them is exactly 114.
All inputs are finite; a program needn't handle non-finite values.
Results may differ from a plain program's by a relative error of at most 0.025.
Values may be sent and summed in bfloat16 or wider, within the bound.
A program may use at most 192 MiB of HBM per device.

v0:
```python
import jax
import jax.numpy as jnp
from jax import lax
from jax.sharding import PartitionSpec as P

HEAD_DIM = 64
HALF = 256


EPSILON = 1e-06
NEGATIVE = -1000000000.0
HIGHEST = lax.Precision.HIGHEST


def from_behind(block, axis, distance):
    devices = range(lax.axis_size(axis))
    route = [(i - distance, i) for i in devices if i - distance in devices]
    return lax.ppermute(block, axis, route)


def rms_norm(inputs, gain_row):
    return (
        inputs * lax.rsqrt(jnp.mean(inputs * inputs, axis=-1, keepdims=True) + EPSILON) * gain_row
    )


def gelu_exact(inputs):
    return jax.nn.gelu(inputs, approximate=False)


def segment_ids(lengths, length):
    boundaries = jnp.cumsum(lengths)
    places = jnp.arange(length, dtype=jnp.int32)
    return jnp.sum((places[:, None] >= boundaries[None, :]).astype(jnp.int32), axis=1)


def bucket_rows(buckets, bias_table):
    onehot = (buckets[:, None] == jnp.arange(bias_table.shape[0], dtype=jnp.int32)[None, :]).astype(
        jnp.float32
    )
    return jnp.dot(onehot, bias_table, precision=HIGHEST)


def toeplitz(vector, length):
    head_count = vector.shape[1]
    flipped = jnp.concatenate([vector[::-1], jnp.zeros((1, head_count), jnp.float32)], axis=0)
    repeated = jnp.tile(flipped.T, (1, length))
    window = repeated[:, length - 1 : length - 1 + length * (2 * length - 1)]
    return window.reshape(head_count, length, 2 * length - 1)[:, :, :length]


def encoder_bias(bias_table, buckets, length):
    return toeplitz(bucket_rows(buckets, bias_table), length)


def decoder_bias(bias_table, buckets, length):
    tail_rows = bucket_rows(buckets, bias_table)
    return toeplitz(
        jnp.concatenate(
            [jnp.zeros((length - 1, bias_table.shape[1]), jnp.float32), tail_rows], axis=0
        ),
        length,
    )


def split_heads(matrix):
    return matrix.reshape(matrix.shape[0], -1, HEAD_DIM)


def merge_heads(stacked):
    return stacked.reshape(stacked.shape[0], -1)


def attend_forward(queries, key_rows, values, position_bias, allowed):
    scores = (
        jnp.einsum("qhd,khd->hqk", queries, key_rows, preferred_element_type=jnp.float32)
        + position_bias
    )
    scores = jnp.where(allowed[None], scores, NEGATIVE)
    row_max = jnp.max(scores, axis=-1, keepdims=True)
    log_total = row_max + jnp.log(jnp.sum(jnp.exp(scores - row_max), axis=-1, keepdims=True))
    attn_probs = jnp.exp(scores - log_total).astype(jnp.bfloat16)
    mixture = jnp.einsum("hqk,khd->qhd", attn_probs, values, preferred_element_type=jnp.float32)
    return (mixture.astype(jnp.bfloat16), log_total)


def attend_backward(queries, key_rows, values, position_bias, allowed, log_total, d_mixture):
    scores = (
        jnp.einsum("qhd,khd->hqk", queries, key_rows, preferred_element_type=jnp.float32)
        + position_bias
    )
    scores = jnp.where(allowed[None], scores, NEGATIVE)
    probs_full = jnp.exp(scores - log_total)
    attn_probs = probs_full.astype(jnp.bfloat16)
    d_probs = jnp.einsum("qhd,khd->hqk", d_mixture, values, preferred_element_type=jnp.float32)
    delta_row = jnp.sum(d_probs * probs_full, axis=-1, keepdims=True)
    d_scores = (probs_full * (d_probs - delta_row)).astype(jnp.bfloat16)
    d_queries = jnp.einsum(
        "hqk,khd->qhd", d_scores, key_rows, preferred_element_type=jnp.float32
    ).astype(jnp.bfloat16)
    d_keys = jnp.einsum(
        "hqk,qhd->khd", d_scores, queries, preferred_element_type=jnp.float32
    ).astype(jnp.bfloat16)
    d_values = jnp.einsum(
        "hqk,qhd->khd", attn_probs, d_mixture, preferred_element_type=jnp.float32
    ).astype(jnp.bfloat16)
    return (d_queries, d_keys, d_values, d_scores)


def spread_rows(normed):
    return lax.all_gather(normed, "tensor", axis=1, tiled=True)


def collect_rows(partial_sums):
    return lax.psum_scatter(partial_sums, "tensor", scatter_dimension=1, tiled=True)


def spread_grads(grad_rows):
    return lax.all_gather(grad_rows, "tensor", axis=1, tiled=True)


def collect_grads(partial_grads):
    return lax.psum_scatter(partial_grads, "tensor", scatter_dimension=1, tiled=True)


def norm_spread(residual, gain_row):
    normed = rms_norm(residual, gain_row).astype(jnp.bfloat16)
    return spread_rows(normed).reshape(-1, residual.shape[-1])


def branch_add(residual, product):
    return residual + collect_rows(product.reshape(residual.shape[0], -1, product.shape[-1]))


def norm_back(residual, gain_row, partial_grads):
    d_normed = collect_grads(partial_grads.reshape(residual.shape[0], -1, partial_grads.shape[-1]))
    unused, pull_back = jax.vjp(rms_norm, residual, gain_row)
    d_residual, d_gain = pull_back(d_normed)
    return (d_residual, d_gain)


def self_forward(residual, gain_row, projections, position_bias, allowed):
    w_query, w_key, w_value, w_out = projections
    hidden = norm_spread(residual, gain_row)
    queries = jnp.dot(hidden, w_query, preferred_element_type=jnp.float32).astype(jnp.bfloat16)
    key_rows = jnp.dot(hidden, w_key, preferred_element_type=jnp.float32).astype(jnp.bfloat16)
    values = jnp.dot(hidden, w_value, preferred_element_type=jnp.float32).astype(jnp.bfloat16)
    mixture, log_total = attend_forward(
        split_heads(queries), split_heads(key_rows), split_heads(values), position_bias, allowed
    )
    mixture = merge_heads(mixture)
    result = branch_add(residual, jnp.dot(mixture, w_out, preferred_element_type=jnp.float32))
    return (result, (hidden, queries, key_rows, values, mixture, log_total))


def self_backward(residual, gain_row, projections, position_bias, allowed, saved, d_result):
    w_query, w_key, w_value, w_out = projections
    hidden, queries, key_rows, values, mixture, log_total = saved
    d_branch = spread_grads(d_result.astype(jnp.bfloat16)).reshape(hidden.shape[0], -1)
    g_out = jnp.einsum("lc,ld->cd", mixture, d_branch, preferred_element_type=jnp.float32)
    d_mixture = jnp.einsum("ld,cd->lc", d_branch, w_out, preferred_element_type=jnp.float32).astype(
        jnp.bfloat16
    )
    d_queries, d_keys, d_values, d_scores = attend_backward(
        split_heads(queries),
        split_heads(key_rows),
        split_heads(values),
        position_bias,
        allowed,
        log_total,
        split_heads(d_mixture),
    )
    d_queries = merge_heads(d_queries)
    d_keys = merge_heads(d_keys)
    d_values = merge_heads(d_values)
    g_query = jnp.einsum("ld,lc->dc", hidden, d_queries, preferred_element_type=jnp.float32)
    g_key = jnp.einsum("ld,lc->dc", hidden, d_keys, preferred_element_type=jnp.float32)
    g_value = jnp.einsum("ld,lc->dc", hidden, d_values, preferred_element_type=jnp.float32)
    d_hidden = jnp.einsum("lc,dc->ld", d_queries, w_query, preferred_element_type=jnp.float32)
    d_hidden = d_hidden + jnp.einsum("lc,dc->ld", d_keys, w_key, preferred_element_type=jnp.float32)
    d_hidden = d_hidden + jnp.einsum(
        "lc,dc->ld", d_values, w_value, preferred_element_type=jnp.float32
    )
    d_residual, d_gain = norm_back(residual, gain_row, d_hidden)
    return (d_result + d_residual, d_gain, (g_query, g_key, g_value, g_out), d_scores)


def feed_forward(residual, gain_row, w_inner, w_outer):
    hidden = norm_spread(residual, gain_row)
    inner_sum = jnp.dot(hidden, w_inner, preferred_element_type=jnp.float32)
    active = gelu_exact(inner_sum).astype(jnp.bfloat16)
    result = branch_add(residual, jnp.dot(active, w_outer, preferred_element_type=jnp.float32))
    return (result, (hidden, inner_sum, active))


def feed_backward(residual, gain_row, w_inner, w_outer, saved, d_result):
    hidden, inner_sum, active = saved
    d_branch = spread_grads(d_result.astype(jnp.bfloat16)).reshape(hidden.shape[0], -1)
    g_outer = jnp.einsum("lf,ld->fd", active, d_branch, preferred_element_type=jnp.float32)
    d_active = jnp.einsum("ld,fd->lf", d_branch, w_outer, preferred_element_type=jnp.float32)
    unused, pull_back = jax.vjp(gelu_exact, inner_sum)
    d_inner = pull_back(d_active)[0].astype(jnp.bfloat16)
    g_inner = jnp.einsum("ld,lf->df", hidden, d_inner, preferred_element_type=jnp.float32)
    d_hidden = jnp.einsum("lf,df->ld", d_inner, w_inner, preferred_element_type=jnp.float32)
    d_residual, d_gain = norm_back(residual, gain_row, d_hidden)
    return (d_result + d_residual, d_gain, (g_inner, g_outer))


def encoder_forward(row_block, lengths, weights, gain_rows, bias_table, buckets):
    w_pair, w_value, w_out, first_cross, second_cross, w_inner, w_outer = weights
    length = 2 * HALF
    segment = segment_ids(lengths, length)
    allowed = segment[:, None] == segment[None, :]
    position_bias = encoder_bias(bias_table, buckets, length)
    projections = (w_pair[0], w_pair[1], w_value, w_out)
    resid_in = row_block.astype(jnp.float32)
    resid_mid, saved_attn = self_forward(
        resid_in, gain_rows[0], projections, position_bias, allowed
    )
    resid_top, saved_feed = feed_forward(resid_mid, gain_rows[1], w_inner, w_outer)
    encoded = norm_spread(resid_top, gain_rows[2])
    cross_keys = jnp.dot(encoded, first_cross, preferred_element_type=jnp.float32).astype(
        jnp.bfloat16
    )
    cross_values = jnp.dot(encoded, second_cross, preferred_element_type=jnp.float32).astype(
        jnp.bfloat16
    )
    return (
        (cross_keys, cross_values),
        (resid_in, resid_mid, resid_top, saved_attn, saved_feed, encoded, position_bias, allowed),
    )


def encoder_backward(weights, gain_rows, bias_table, buckets, saved, d_cross_keys, d_cross_values):
    w_pair, w_value, w_out, first_cross, second_cross, w_inner, w_outer = weights
    resid_in, resid_mid, resid_top, saved_attn, saved_feed, encoded, position_bias, allowed = saved
    length = 2 * HALF
    projections = (w_pair[0], w_pair[1], w_value, w_out)
    g_first = jnp.einsum("ld,lc->dc", encoded, d_cross_keys, preferred_element_type=jnp.float32)
    g_second = jnp.einsum("ld,lc->dc", encoded, d_cross_values, preferred_element_type=jnp.float32)
    d_encoded = jnp.einsum(
        "lc,dc->ld", d_cross_keys, first_cross, preferred_element_type=jnp.float32
    )
    d_encoded = d_encoded + jnp.einsum(
        "lc,dc->ld", d_cross_values, second_cross, preferred_element_type=jnp.float32
    )
    d_top, gain_top = norm_back(resid_top, gain_rows[2], d_encoded)
    d_mid, gain_mid, feed_grads = feed_backward(
        resid_mid, gain_rows[1], w_inner, w_outer, saved_feed, d_top
    )
    d_input, gain_in, attn_grads, d_scores = self_backward(
        resid_in, gain_rows[0], projections, position_bias, allowed, saved_attn, d_mid
    )
    unused, pull_back = jax.vjp(
        lambda bias_vals: encoder_bias(bias_vals, buckets, length), bias_table
    )
    g_table = pull_back(d_scores.astype(jnp.float32))[0]
    grad_set = (
        jnp.stack([attn_grads[0], attn_grads[1]]),
        attn_grads[2],
        attn_grads[3],
        g_first,
        g_second,
        feed_grads[0],
        feed_grads[1],
        jnp.stack([gain_in, gain_mid, gain_top]),
        g_table,
    )
    return (d_input, grad_set)


def decoder_pass(
    row_block,
    dec_length,
    enc_length,
    weights,
    gain_rows,
    bias_table,
    buckets,
    cross_keys,
    cross_values,
):
    w_pair, w_value, w_out, first_cross, second_cross, w_inner, w_outer = weights
    projections = (w_pair[0], w_pair[1], w_value, w_out)
    dec_rows = row_block[0:1].astype(jnp.float32)
    cotangent = row_block[1:2].astype(jnp.float32)
    dec_seg = segment_ids(dec_length, HALF)
    enc_seg = segment_ids(enc_length, 2 * HALF)
    places = jnp.arange(HALF, dtype=jnp.int32)
    allowed = (dec_seg[:, None] == dec_seg[None, :]) & (places[:, None] >= places[None, :])
    cross_allowed = dec_seg[:, None] == enc_seg[None, :]
    position_bias = decoder_bias(bias_table, buckets, HALF)
    resid_mid, saved_attn = self_forward(
        dec_rows, gain_rows[0], projections, position_bias, allowed
    )
    cross_hidden = norm_spread(resid_mid, gain_rows[1])
    cross_queries = jnp.dot(cross_hidden, first_cross, preferred_element_type=jnp.float32).astype(
        jnp.bfloat16
    )
    cross_mixture, cross_total = attend_forward(
        split_heads(cross_queries),
        split_heads(cross_keys),
        split_heads(cross_values),
        0.0,
        cross_allowed,
    )
    cross_mixture = merge_heads(cross_mixture)
    resid_cross = branch_add(
        resid_mid,
        jnp.einsum("lc,dc->ld", cross_mixture, second_cross, preferred_element_type=jnp.float32),
    )
    resid_top, saved_feed = feed_forward(resid_cross, gain_rows[2], w_inner, w_outer)
    d_cross, gain_top, feed_grads = feed_backward(
        resid_cross, gain_rows[2], w_inner, w_outer, saved_feed, cotangent
    )
    d_branch = spread_grads(d_cross.astype(jnp.bfloat16)).reshape(cross_hidden.shape[0], -1)
    g_second = jnp.einsum("ld,lc->dc", d_branch, cross_mixture, preferred_element_type=jnp.float32)
    d_mixture = jnp.einsum(
        "ld,dc->lc", d_branch, second_cross, preferred_element_type=jnp.float32
    ).astype(jnp.bfloat16)
    d_queries, d_keys, d_values, unused_scores = attend_backward(
        split_heads(cross_queries),
        split_heads(cross_keys),
        split_heads(cross_values),
        0.0,
        cross_allowed,
        cross_total,
        split_heads(d_mixture),
    )
    d_queries = merge_heads(d_queries)
    g_first = jnp.einsum("ld,lc->dc", cross_hidden, d_queries, preferred_element_type=jnp.float32)
    d_mid_norm, gain_mid = norm_back(
        resid_mid,
        gain_rows[1],
        jnp.einsum("lc,dc->ld", d_queries, first_cross, preferred_element_type=jnp.float32),
    )
    d_mid = d_cross + d_mid_norm
    d_input, gain_in, attn_grads, d_scores = self_backward(
        dec_rows, gain_rows[0], projections, position_bias, allowed, saved_attn, d_mid
    )
    unused, pull_back = jax.vjp(
        lambda bias_vals: decoder_bias(bias_vals, buckets, HALF), bias_table
    )
    g_table = pull_back(d_scores.astype(jnp.float32))[0]
    grad_set = (
        jnp.stack([attn_grads[0], attn_grads[1]]),
        attn_grads[2],
        attn_grads[3],
        g_first,
        g_second,
        feed_grads[0],
        feed_grads[1],
        jnp.stack([gain_in, gain_mid, gain_top]),
        g_table,
    )
    out_rows = jnp.concatenate([resid_top, d_input], axis=0)
    return (merge_heads(d_keys), merge_heads(d_values), out_rows, grad_set)


def add_sets(first_set, second_set):
    return tuple((left + right for left, right in zip(first_set, second_set)))


def shards(
    section_rows,
    enc_lengths,
    dec_lengths,
    enc_buckets,
    dec_buckets,
    norm_gains,
    rel_bias,
    query_key_w,
    value_w,
    attn_out_w,
    cross_first,
    cross_second,
    ff_in,
    ff_out,
):
    on_encoder = lax.axis_index("pipe") == 0
    gain_rows = norm_gains[0]
    bias_table = rel_bias[0]
    totals = None
    row_results = []
    for micro_step in range(section_rows.shape[1]):
        weights = (
            lax.all_gather(query_key_w[0], "dp", axis=1, tiled=True),
            lax.all_gather(value_w[0], "dp", axis=0, tiled=True),
            lax.all_gather(attn_out_w[0], "dp", axis=1, tiled=True),
            lax.all_gather(cross_first[0], "dp", axis=0, tiled=True),
            lax.all_gather(cross_second[0], "dp", axis=0, tiled=True),
            lax.all_gather(ff_in[0], "dp", axis=0, tiled=True),
            lax.all_gather(ff_out[0], "dp", axis=1, tiled=True),
        )
        row_block = section_rows[0, micro_step]
        enc_length = enc_lengths[micro_step]
        dec_length = dec_lengths[micro_step]
        cross_pair, enc_saved = encoder_forward(
            row_block, enc_length, weights, gain_rows, bias_table, enc_buckets
        )
        cross_keys, cross_values = from_behind((cross_pair[0], cross_pair[1]), "pipe", 1)
        d_keys, d_values, dec_output, dec_grads = decoder_pass(
            row_block,
            dec_length,
            enc_length,
            weights,
            gain_rows,
            bias_table,
            dec_buckets,
            cross_keys,
            cross_values,
        )
        back_keys, back_values = from_behind((d_keys, d_values), "pipe", -1)
        enc_input, enc_grads = encoder_backward(
            weights, gain_rows, bias_table, enc_buckets, enc_saved, back_keys, back_values
        )
        row_results.append(jnp.where(on_encoder, enc_input, dec_output))
        grad_set = tuple(
            (jnp.where(on_encoder, left, right) for left, right in zip(enc_grads, dec_grads))
        )
        grad_shards = (
            lax.psum_scatter(
                grad_set[0].astype(jnp.bfloat16), "dp", scatter_dimension=1, tiled=True
            ).astype(jnp.float32),
            lax.psum_scatter(
                grad_set[1].astype(jnp.bfloat16), "dp", scatter_dimension=0, tiled=True
            ).astype(jnp.float32),
            lax.psum_scatter(
                grad_set[2].astype(jnp.bfloat16), "dp", scatter_dimension=1, tiled=True
            ).astype(jnp.float32),
            lax.psum_scatter(
                grad_set[3].astype(jnp.bfloat16), "dp", scatter_dimension=0, tiled=True
            ).astype(jnp.float32),
            lax.psum_scatter(
                grad_set[4].astype(jnp.bfloat16), "dp", scatter_dimension=0, tiled=True
            ).astype(jnp.float32),
            lax.psum_scatter(
                grad_set[5].astype(jnp.bfloat16), "dp", scatter_dimension=0, tiled=True
            ).astype(jnp.float32),
            lax.psum_scatter(
                grad_set[6].astype(jnp.bfloat16), "dp", scatter_dimension=1, tiled=True
            ).astype(jnp.float32),
            lax.psum_scatter(
                grad_set[7].astype(jnp.bfloat16), "dp", scatter_dimension=1, tiled=True
            ).astype(jnp.float32),
            lax.psum_scatter(
                grad_set[8].astype(jnp.bfloat16), "dp", scatter_dimension=0, tiled=True
            ).astype(jnp.float32),
        )
        totals = grad_shards if totals is None else add_sets(totals, grad_shards)
    gain_total = lax.psum(totals[7], "tensor")
    section_out = jnp.stack(row_results)[None]
    return (
        section_out,
        gain_total[None],
        totals[8][None],
        totals[0][None],
        totals[1][None],
        totals[2][None],
        totals[3][None],
        totals[4][None],
        totals[5][None],
        totals[6][None],
    )


def solution(mesh):
    return jax.shard_map(
        shards,
        mesh=mesh,
        in_specs=(
            P("pipe", "dp", None, "tensor", None),
            P("dp", None),
            P("dp", None),
            P(),
            P(),
            P("pipe", None, None),
            P("pipe", None, "tensor"),
            P("pipe", None, "dp", "tensor"),
            P("pipe", "dp", "tensor"),
            P("pipe", "tensor", "dp"),
            P("pipe", "dp", "tensor"),
            P("pipe", "dp", "tensor"),
            P("pipe", "dp", "tensor"),
            P("pipe", "tensor", "dp"),
        ),
        out_specs=(
            P("pipe", "dp", None, "tensor", None),
            P("pipe", None, "dp"),
            P("pipe", "dp", "tensor"),
            P("pipe", None, "dp", "tensor"),
            P("pipe", "dp", "tensor"),
            P("pipe", "tensor", "dp"),
            P("pipe", "dp", "tensor"),
            P("pipe", "dp", "tensor"),
            P("pipe", "dp", "tensor"),
            P("pipe", "tensor", "dp"),
        ),
        check_vma=False,
    )
```

profile of v0, /device:TPU:8, one launch (start us, length us, event | category | flops | bytes accessed | tf_op | source)
XLA Modules:
  0.0 1456.0 jit_solution(2707273798406188477)
XLA Ops:
  11.9 17.9 %all_gather.100 = bf16[2,256,768]{2,1,0:T(8,128)(2,1)S(1)} all-gather(bf16[2,64,768]{2,1,0:T(8,128)(2,1)S(1)} %get-tuple-element.124), channel_id=1, replica_groups=mesh['pipe'=2,'dp'=4,'tensor'=4] {'tensor'}, dimensions={1}, use_global_device_ids=true | all-gather | bytes 983040 | tf_op jit(solution)/shard_map/all_gather | solution.py:111
  109.0 31.0 %all_gather.114 = bf16[2,256,768]{2,1,0:T(8,128)(2,1)S(1)} all-gather(bf16[2,64,768]{2,1,0:T(8,128)(2,1)} %get-tuple-element.125), channel_id=1, replica_groups=mesh['pipe'=2,'dp'=4,'tensor'=4] {'tensor'}, dimensions={1}, use_global_device_ids=true | all-gather | bytes 983040 | tf_op jit(solution)/shard_map/all_gather | solution.py:111
  166.0 20.0 %all_gather.94 = bf16[1,256,768]{2,1,0:T(8,128)(2,1)} all-gather(bf16[1,64,768]{2,1,0:T(8,128)(2,1)S(1)} %get-tuple-element.126), channel_id=1, replica_groups=mesh['pipe'=2,'dp'=4,'tensor'=4] {'tensor'}, dimensions={1}, use_global_device_ids=true | all-gather | bytes 491520 | tf_op jit(solution)/shard_map/all_gather | solution.py:111
  209.1 27.8 %all_gather.101 = bf16[2,256,768]{2,1,0:T(8,128)(2,1)} all-gather(bf16[2,64,768]{2,1,0:T(8,128)(2,1)S(1)} %multiply_convert_fusion.13), channel_id=1, replica_groups=mesh['pipe'=2,'dp'=4,'tensor'=4] {'tensor'}, dimensions={1}, use_global_device_ids=true | all-gather | bytes 983040 | tf_op jit(solution)/shard_map/all_gather | solution.py:111
  265.6 18.7 %all_gather.98 = bf16[1,256,768]{2,1,0:T(8,128)(2,1)S(1)} all-gather(bf16[1,64,768]{2,1,0:T(8,128)(2,1)S(1)} %multiply_convert_fusion.17), channel_id=1, replica_groups=mesh['pipe'=2,'dp'=4,'tensor'=4] {'tensor'}, dimensions={1}, use_global_device_ids=true | all-gather | bytes 491520 | tf_op jit(solution)/shard_map/all_gather | solution.py:111
  290.6 17.4 %all_gather.104 = bf16[2,256,768]{2,1,0:T(8,128)(2,1)S(1)} all-gather(bf16[2,64,768]{2,1,0:T(8,128)(2,1)S(1)} %multiply_convert_fusion.12), channel_id=1, replica_groups=mesh['pipe'=2,'dp'=4,'tensor'=4] {'tensor'}, dimensions={1}, use_global_device_ids=true | all-gather | bytes 983040 | tf_op jit(solution)/shard_map/all_gather | solution.py:111
  324.3 18.9 %all-gather.7 = bf16[1,1,1,256,768]{4,3,2,1,0:T(8,128)(2,1)} all-gather(bf16[1,1,1,64,768]{4,3,2,1,0:T(8,128)(2,1)S(1)} %get-tuple-element.129), channel_id=9, replica_groups=mesh['pipe'=2,'dp'=4,'tensor'=4] {'tensor'}, dimensions={3}, use_global_device_ids=true | all-gather | bytes 491520 | tf_op jit(solution)/shard_map/all_gather | solution.py:119
  392.5 16.2 %reduce-scatter.65.cloned.1.call-done = f32[1,64,768]{2,1,0:T(8,128)} async-done(((f32[1,256,768]{2,1,0:T(8,128)}), f32[1,64,768]{2,1,0:T(8,128)}) %reduce-scatter.65.cloned.1.call-update) | async-done | bytes 196624 | tf_op jit(solution)/shard_map/reduce_scatter | solution.py:123
  411.5 22.1 %reduce-scatter.79.cloned.1.call-done = f32[1,64,768]{2,1,0:T(8,128)} async-done(((f32[1,256,768]{2,1,0:T(8,128)}), f32[1,64,768]{2,1,0:T(8,128)}) %reduce-scatter.79.cloned.1.call-update) | async-done | bytes 196624 | tf_op jit(solution)/shard_map/reduce_scatter | solution.py:115
  466.6 34.4 %reduce-scatter.67.cloned.1.call-done = f32[2,64,768]{2,1,0:T(8,128)} async-done(((f32[2,256,768]{2,1,0:T(8,128)}), f32[2,64,768]{2,1,0:T(8,128)}) %reduce-scatter.67.cloned.1.call-update) | async-done | bytes 393232 | tf_op jit(solution)/shard_map/reduce_scatter | solution.py:123
  504.9 17.4 %all_gather.109 = bf16[2,256,768]{2,1,0:T(8,128)(2,1)S(1)} all-gather(bf16[2,64,768]{2,1,0:T(8,128)(2,1)S(1)} %fusion.221), channel_id=1, replica_groups=mesh['pipe'=2,'dp'=4,'tensor'=4] {'tensor'}, dimensions={1}, use_global_device_ids=true | all-gather | bytes 983040 | tf_op jit(solution)/shard_map/all_gather | solution.py:119
  532.0 30.7 %reduce-scatter.69.cloned.1.call-done = f32[2,64,768]{2,1,0:T(8,128)} async-done(((f32[2,256,768]{2,1,0:T(8,128)}), f32[2,64,768]{2,1,0:T(8,128)}) %reduce-scatter.69.cloned.1.call-update) | async-done | bytes 393232 | tf_op jit(solution)/shard_map/reduce_scatter | solution.py:123
  564.7 27.1 %all_gather.115 = bf16[2,256,768]{2,1,0:T(8,128)(2,1)S(1)} all-gather(bf16[2,64,768]{2,1,0:T(8,128)(2,1)S(1)} %get-tuple-element.137), channel_id=1, replica_groups=mesh['pipe'=2,'dp'=4,'tensor'=4] {'tensor'}, dimensions={1}, use_global_device_ids=true | all-gather | bytes 983040 | tf_op jit(solution)/shard_map/all_gather | solution.py:111
  604.0 18.5 %all_gather.113 = bf16[1,256,768]{2,1,0:T(8,128)(2,1)S(1)} all-gather(bf16[1,64,768]{2,1,0:T(8,128)(2,1)S(1)} %get-tuple-element.138), channel_id=1, replica_groups=mesh['pipe'=2,'dp'=4,'tensor'=4] {'tensor'}, dimensions={1}, use_global_device_ids=true | all-gather | bytes 491520 | tf_op jit(solution)/shard_map/all_gather | solution.py:111
  641.0 18.6 %all_gather.116 = bf16[2,256,768]{2,1,0:T(8,128)(2,1)S(1)} all-gather(bf16[2,64,768]{2,1,0:T(8,128)(2,1)S(1)} %multiply_convert_fusion.10), channel_id=1, replica_groups=mesh['pipe'=2,'dp'=4,'tensor'=4] {'tensor'}, dimensions={1}, use_global_device_ids=true | all-gather | bytes 983040 | tf_op jit(solution)/shard_map/all_gather | solution.py:111
  672.6 18.5 %all-gather.8 = bf16[1,1,1,256,768]{4,3,2,1,0:T(8,128)(2,1)} all-gather(bf16[1,1,1,64,768]{4,3,2,1,0:T(8,128)(2,1)} %get-tuple-element.130), channel_id=10, replica_groups=mesh['pipe'=2,'dp'=4,'tensor'=4] {'tensor'}, dimensions={3}, use_global_device_ids=true | all-gather | bytes 491520 | tf_op jit(solution)/shard_map/all_gather | solution.py:119
  729.2 15.8 %reduce-scatter.87.cloned.1.call-done = f32[1,64,768]{2,1,0:T(8,128)} async-done(((f32[1,256,768]{2,1,0:T(8,128)}), f32[1,64,768]{2,1,0:T(8,128)}) %reduce-scatter.87.cloned.1.call-update) | async-done | bytes 196624 | tf_op jit(solution)/shard_map/reduce_scatter | solution.py:123
  747.9 21.9 %reduce-scatter.73.cloned.1.call-done = f32[1,64,768]{2,1,0:T(8,128)} async-done(((f32[1,256,768]{2,1,0:T(8,128)}), f32[1,64,768]{2,1,0:T(8,128)}) %reduce-scatter.73.cloned.1.call-update) | async-done | bytes 196624 | tf_op jit(solution)/shard_map/reduce_scatter | solution.py:115
  769.8 24.8 %reduce-scatter.95.cloned.1.call-done = f32[1,64,768]{2,1,0:T(8,128)} async-done(((f32[1,256,768]{2,1,0:T(8,128)}), f32[1,64,768]{2,1,0:T(8,128)}) %reduce-scatter.95.cloned.1.call-update) | async-done | bytes 196624 | tf_op jit(solution)/shard_map/reduce_scatter | solution.py:115
  797.2 15.8 %all_gather.119 = bf16[1,256,768]{2,1,0:T(8,128)(2,1)S(1)} all-gather(bf16[1,64,768]{2,1,0:T(8,128)(2,1)S(1)} %get-tuple-element.123), channel_id=1, replica_groups=mesh['pipe'=2,'dp'=4,'tensor'=4] {'tensor'}, dimensions={1}, use_global_device_ids=true | all-gather | bytes 491520 | tf_op jit(solution)/shard_map/all_gather | solution.py:119
  849.4 18.5 %all_gather.111 = bf16[1,256,768]{2,1,0:T(8,128)(2,1)S(1)} all-gather(bf16[1,64,768]{2,1,0:T(8,128)(2,1)} %get-tuple-element.95), channel_id=1, replica_groups=mesh['pipe'=2,'dp'=4,'tensor'=4] {'tensor'}, dimensions={1}, use_global_device_ids=true | all-gather | bytes 491520 | tf_op jit(solution)/shard_map/all_gather | solution.py:119
  910.5 15.9 %all_gather.120 = bf16[2,256,768]{2,1,0:T(8,128)(2,1)S(1)} all-gather(bf16[2,64,768]{2,1,0:T(8,128)(2,1)S(1)} %fusion.222), channel_id=1, replica_groups=mesh['pipe'=2,'dp'=4,'tensor'=4] {'tensor'}, dimensions={1}, use_global_device_ids=true | all-gather | bytes 983040 | tf_op jit(solution)/shard_map/all_gather | solution.py:119
  982.5 23.5 %reduce-scatter.107.cloned.1.call-done = bf16[192,192]{1,0:T(8,128)(2,1)} async-done(((bf16[768,192]{1,0:T(8,128)(2,1)}), bf16[192,192]{1,0:T(8,128)(2,1)}) %reduce-scatter.107.cloned.1.call-update) | async-done | bytes 73744 | tf_op jit(solution)/shard_map/reduce_scatter | solution.py:431
  1029.9 24.9 %reduce-scatter.99.cloned.1.call-done = f32[1,64,768]{2,1,0:T(8,128)} async-done(((f32[1,256,768]{2,1,0:T(8,128)}), f32[1,64,768]{2,1,0:T(8,128)}) %reduce-scatter.99.cloned.1.call-update) | async-done | bytes 196624 | tf_op jit(solution)/shard_map/reduce_scatter | solution.py:123
  1063.8 20.5 %reduce-scatter.131.cloned.1.call-done = bf16[192,768]{1,0:T(8,128)(2,1)} async-done(((bf16[768,768]{1,0:T(8,128)(2,1)}), bf16[192,768]{1,0:T(8,128)(2,1)}) %reduce-scatter.131.cloned.1.call-update) | async-done | bytes 294928
  1086.2 34.5 %reduce-scatter.91.cloned.1.call-done = f32[2,64,768]{2,1,0:T(8,128)} async-done(((f32[2,256,768]{2,1,0:T(8,128)}), f32[2,64,768]{2,1,0:T(8,128)}) %reduce-scatter.91.cloned.1.call-update) | async-done | bytes 393232 | tf_op jit(solution)/shard_map/reduce_scatter | solution.py:123
  1126.5 17.4 %all_gather.110 = bf16[2,256,768]{2,1,0:T(8,128)(2,1)S(1)} all-gather(bf16[2,64,768]{2,1,0:T(8,128)(2,1)S(1)} %get-tuple-element.89), channel_id=1, replica_groups=mesh['pipe'=2,'dp'=4,'tensor'=4] {'tensor'}, dimensions={1}, use_global_device_ids=true | all-gather | bytes 983040 | tf_op jit(solution)/shard_map/all_gather | solution.py:119
  1147.7 18.4 %all_gather.121 = bf16[2,256,768]{2,1,0:T(8,128)(2,1)S(1)} all-gather(bf16[2,64,768]{2,1,0:T(8,128)(2,1)} %get-tuple-element.135), channel_id=1, replica_groups=mesh['pipe'=2,'dp'=4,'tensor'=4] {'tensor'}, dimensions={1}, use_global_device_ids=true | all-gather | bytes 983040 | tf_op jit(solution)/shard_map/all_gather | solution.py:119
  1322.8 34.1 %reduce-scatter.93.cloned.1.call-done = f32[2,64,768]{2,1,0:T(8,128)} async-done(((f32[2,256,768]{2,1,0:T(8,128)}), f32[2,64,768]{2,1,0:T(8,128)}) %reduce-scatter.93.cloned.1.call-update) | async-done | bytes 393232 | tf_op jit(solution)/shard_map/reduce_scatter | solution.py:123
  1356.9 36.5 %reduce-scatter.71.cloned.1.call-done = f32[2,64,768]{2,1,0:T(8,128)} async-done(((f32[2,256,768]{2,1,0:T(8,128)}), f32[2,64,768]{2,1,0:T(8,128)}) %reduce-scatter.71.cloned.1.call-update) | async-done | bytes 393232 | tf_op jit(solution)/shard_map/reduce_scatter | solution.py:123
  1399.4 16.4 %reduce-scatter.117.cloned.1.call-done = bf16[192,3]{1,0:T(8,128)(2,1)} async-done(((bf16[768,3]{1,0:T(8,128)(2,1)}), bf16[192,3]{1,0:T(8,128)(2,1)}) %reduce-scatter.117.cloned.1.call-update) | async-done | bytes 1168
  1416.6 21.4 %reduce-scatter.119.cloned.1.call-done = bf16[192,3]{1,0:T(8,128)(2,1)} async-done(((bf16[768,3]{1,0:T(8,128)(2,1)}), bf16[192,3]{1,0:T(8,128)(2,1)}) %reduce-scatter.119.cloned.1.call-update) | async-done | bytes 1168
  (955 shorter events, 721.2 us)
Async XLA Ops:
  8.0 197.6 %reduce-scatter.59.cloned.1.call-start = ((), (), s32[]{:S(2)}) async-start(), calls=%async_computation.39 | async-start | bytes 1966080 | tf_op jit(solution)/shard_map/reduce_scatter | solution.py:115
  106.6 99.0 %reduce-scatter.81.cloned.1.call-start = ((), (), s32[]{:S(2)}) async-start(), calls=%async_computation.50 | async-start | bytes 1966080 | tf_op jit(solution)/shard_map/reduce_scatter | solution.py:115
  150.8 93.2 %all-gather.14.cloned.1.call-start = ((), (), s32[]{:S(2)}) async-start(), calls=%async_computation.69 | async-start | bytes 1474560 | tf_op jit(solution)/shard_map/all_gather | solution.py:393
  151.4 111.9 %reduce-scatter.57.cloned.1.call-start = ((), (), s32[]{:S(2)}) async-start(), calls=%async_computation.38 | async-start | bytes 983040 | tf_op jit(solution)/shard_map/reduce_scatter | solution.py:115
  247.6 113.7 %reduce-scatter.63.cloned.1.call-start = ((), (), s32[]{:S(2)}) async-start(), calls=%async_computation.41 | async-start | bytes 983040 | tf_op jit(solution)/shard_map/reduce_scatter | solution.py:115
  320.0 88.6 %reduce-scatter.65.cloned.1.call-start = ((), (), s32[]{:S(2)}) async-start(), calls=%async_computation.42 | async-start | bytes 983040 | tf_op jit(solution)/shard_map/reduce_scatter | solution.py:123
  392.4 108.6 %reduce-scatter.67.cloned.1.call-start = ((), (), s32[]{:S(2)}) async-start(), calls=%async_computation.43 | async-start | bytes 1966080 | tf_op jit(solution)/shard_map/reduce_scatter | solution.py:123
  466.6 96.1 %reduce-scatter.69.cloned.1.call-start = ((), (), s32[]{:S(2)}) async-start(), calls=%async_computation.44 | async-start | bytes 1966080 | tf_op jit(solution)/shard_map/reduce_scatter | solution.py:123
  531.9 106.9 %reduce-scatter.83.cloned.1.call-start = ((), (), s32[]{:S(2)}) async-start(), calls=%async_computation.51 | async-start | bytes 1966080 | tf_op jit(solution)/shard_map/reduce_scatter | solution.py:115
  599.3 99.5 %reduce-scatter.85.cloned.1.call-start = ((), (), s32[]{:S(2)}) async-start(), calls=%async_computation.52 | async-start | bytes 983040 | tf_op jit(solution)/shard_map/reduce_scatter | solution.py:115
  728.0 151.5 %reduce-scatter.97.cloned.1.call-start = ((), (), s32[]{:S(2)}) async-start(), calls=%async_computation.58 | async-start | bytes 983040 | tf_op jit(solution)/shard_map/reduce_scatter | solution.py:123
  817.9 88.7 %reduce-scatter.89.cloned.1.call-start = ((), (), s32[]{:S(2)}) async-start(), calls=%async_computation.54 | async-start | bytes 1966080 | tf_op jit(solution)/shard_map/reduce_scatter | solution.py:123
  831.2 113.7 %reduce-scatter.129.cloned.1.call-start = ((), (), s32[]{:S(2)}) async-start(), calls=%async_computation.76 | async-start | bytes 1474560
  838.2 130.4 %reduce-scatter.109.cloned.1.call-start = ((), (), s32[]{:S(2)}) async-start(), calls=%async_computation.64 | async-start | bytes 491520 | tf_op jit(solution)/shard_map/reduce_scatter | solution.py:434
  841.8 126.7 %reduce-scatter.111.cloned.1.call-start = ((), (), s32[]{:S(2)}) async-start(), calls=%async_computation.65 | async-start | bytes 491520 | tf_op jit(solution)/shard_map/reduce_scatter | solution.py:434
  845.6 136.9 %reduce-scatter.105.cloned.1.call-start = ((), (), s32[]{:S(2)}) async-start(), calls=%async_computation.62 | async-start | bytes 491520 | tf_op jit(solution)/shard_map/reduce_scatter | solution.py:431
  849.3 156.7 %reduce-scatter.107.cloned.1.call-start = ((), (), s32[]{:S(2)}) async-start(), calls=%async_computation.63 | async-start | bytes 491520 | tf_op jit(solution)/shard_map/reduce_scatter | solution.py:431
  874.2 155.7 %reduce-scatter.77.cloned.1.call-start = ((), (), s32[]{:S(2)}) async-start(), calls=%async_computation.48 | async-start | bytes 983040 | tf_op jit(solution)/shard_map/reduce_scatter | solution.py:123
  879.4 175.3 %reduce-scatter.99.cloned.1.call-start = ((), (), s32[]{:S(2)}) async-start(), calls=%async_computation.59 | async-start | bytes 983040 | tf_op jit(solution)/shard_map/reduce_scatter | solution.py:123
  903.9 180.5 %reduce-scatter.131.cloned.1.call-start = ((), (), s32[]{:S(2)}) async-start(), calls=%async_computation.77 | async-start | bytes 1474560
  931.6 189.1 %reduce-scatter.91.cloned.1.call-start = ((), (), s32[]{:S(2)}) async-start(), calls=%async_computation.55 | async-start | bytes 1966080 | tf_op jit(solution)/shard_map/reduce_scatter | solution.py:123
  937.3 289.5 %reduce-scatter.113.cloned.1.call-start = ((), (), s32[]{:S(2)}) async-start(), calls=%async_computation.66 | async-start | bytes 1474560 | tf_op jit(solution)/shard_map/reduce_scatter | solution.py:437
  944.8 282.0 %reduce-scatter.115.cloned.1.call-start = ((), (), s32[]{:S(2)}) async-start(), calls=%async_computation.67 | async-start | bytes 1474560 | tf_op jit(solution)/shard_map/reduce_scatter | solution.py:437
  1063.8 243.8 %reduce-scatter.125.cloned.1.call-start = ((), (), s32[]{:S(2)}) async-start(), calls=%async_computation.74 | async-start | bytes 491520
  1177.6 131.1 %reduce-scatter.127.cloned.1.call-start = ((), (), s32[]{:S(2)}) async-start(), calls=%async_computation.75 | async-start | bytes 491520
  1185.0 125.3 %reduce-scatter.101.cloned.1.call-start = ((), (), s32[]{:S(2)}) async-start(), calls=%async_computation.60 | async-start | bytes 491520 | tf_op jit(solution)/shard_map/reduce_scatter | solution.py:425
  1196.1 114.2 %reduce-scatter.103.cloned.1.call-start = ((), (), s32[]{:S(2)}) async-start(), calls=%async_computation.61 | async-start | bytes 491520 | tf_op jit(solution)/shard_map/reduce_scatter | solution.py:425
  1203.5 108.5 %reduce-scatter.123.cloned.1.call-start = ((), (), s32[]{:S(2)}) async-start(), calls=%async_computation.73 | async-start | bytes 737280
  1216.6 103.8 %reduce-scatter.121.cloned.1.call-start = ((), (), s32[]{:S(2)}) async-start(), calls=%async_computation.72 | async-start | bytes 737280
  1225.2 131.7 %reduce-scatter.93.cloned.1.call-start = ((), (), s32[]{:S(2)}) async-start(), calls=%async_computation.56 | async-start | bytes 1966080 | tf_op jit(solution)/shard_map/reduce_scatter | solution.py:123
  1249.0 144.3 %reduce-scatter.71.cloned.1.call-start = ((), (), s32[]{:S(2)}) async-start(), calls=%async_computation.45 | async-start | bytes 1966080 | tf_op jit(solution)/shard_map/reduce_scatter | solution.py:123
  1277.8 138.0 %reduce-scatter.117.cloned.1.call-start = ((), (), s32[]{:S(2)}) async-start(), calls=%async_computation.70 | async-start | bytes 245760
  (262 other events, 3481.5 us)
Sparse Core Ops, SparseCore 0:
  106.7 45.4 reduce-scatter.58
  154.5 42.3 reduce-scatter.80
  205.7 31.3 reduce-scatter.56
  247.7 40.7 reduce-scatter.60
  320.2 29.9 reduce-scatter.62
  384.9 23.6 reduce-scatter.64
  411.0 22.5 reduce-scatter.78
  466.7 34.2 reduce-scatter.66
  527.3 35.3 reduce-scatter.68
  564.8 29.8 reduce-scatter.74
  599.4 39.3 reduce-scatter.82
  672.6 26.1 reduce-scatter.84
  722.4 22.6 reduce-scatter.86
  747.2 22.5 reduce-scatter.72
  771.9 22.5 reduce-scatter.94
  818.0 22.4 reduce-scatter.96
  842.6 40.5 reduce-scatter.88
  885.6 26.5 reduce-scatter.128
  961.6 20.8 reduce-scatter.104
  1008.4 21.4 reduce-scatter.76
  1032.2 22.5 reduce-scatter.98
  1057.5 26.7 reduce-scatter.130
  1086.5 34.1 reduce-scatter.90
  1123.1 25.7 reduce-scatter.112
  1151.7 25.6 reduce-scatter.114
  1203.1 20.8 reduce-scatter.126
  1226.5 20.8 reduce-scatter.100
  1250.4 20.8 reduce-scatter.102
  1273.7 22.0 reduce-scatter.122
  1298.3 22.0 reduce-scatter.120
  1322.7 34.1 reduce-scatter.92
  1359.0 34.2 reduce-scatter.70
  (4 shorter events, 82.9 us)
Sparse Core Ops, SparseCore 1:
  152.3 18.0 all-gather.11
  171.8 17.3 all-gather.13
  1396.0 19.7 reduce-scatter.116
  1418.2 19.7 reduce-scatter.118
where the time goes:
time: 1470 us; the launch traced here: 1460 us
  blocking collectives  465 us (32%)
  waiting for transfers between devices  447 us (30%)
  matrix products  193 us (13%)
  local copies, waits for them, and re-layouts  185 us (13%)
  other arithmetic  129 us (9%)
  between operations  19.6 us (1%)
  starting transfers between devices  17.1 us (1%)
    all_gather x12, blocking collectives, spread_rows(): return lax.all_gather(normed, 'tensor', axis=1, tiled=True)  241 us
    reduce_scatter x12, waiting for transfers between devices, collect_grads(): lax.psum_scatter(partial_grads, 'tensor', scatter_dimension=1, tiled=True)  232 us
    all_gather x10, blocking collectives, spread_grads(): return lax.all_gather(grad_rows, 'tensor', axis=1, tiled=True)  171 us
    unnamed x534, local copies, waits for them, and re-layouts  105 us
    reduce_scatter x10, waiting for transfers between devices, collect_rows(): lax.psum_scatter(partial_sums, 'tensor', scatter_dimension=1, tiled=True)  93.5 us
    unnamed x48, waiting for transfers between devices  67.1 us
    reshape x6, local copies, waits for them, and re-layouts, toeplitz(): return window.reshape(head_count, length, 2 * length - 1)[:, :, :length]  36.4 us
    reduce_scatter x2, waiting for transfers between devices, shards(): lax.psum_scatter(grad_set[3].astype(jnp.bfloat16), 'dp', scatter_dimensio...  35.8 us
  transfers between devices with their start and end apart: 48, of which 29 were waited for; matrix products, arithmetic and copies ran while one was open for 26% of the time, Pallas kernels for 0%

commit v1 on v0

v1 whole, which is shorter than its diff:
```python
import functools

import jax
import jax.numpy as jnp
from jax import lax
from jax.experimental import pallas as pl
from jax.experimental.pallas import tpu as pltpu
from jax.sharding import PartitionSpec as P

MESH = pl.DeviceIdType.MESH
F32 = jnp.float32
BF16 = jnp.bfloat16
EPSILON = 1e-06
NEGATIVE = -1000000000.0
HEAD_DIM = 64
CORES = 2
LANES = 128
VMEM_LIMIT = 60 << 20
ANY = pl.BlockSpec(memory_space=pl.ANY)
VMEM = pl.BlockSpec(memory_space=pltpu.VMEM)


def nn(a, b):
    return lax.dot_general(a, b, (((1,), (0,)), ((), ())), preferred_element_type=F32)


def nt(a, b):
    return lax.dot_general(a, b, (((1,), (1,)), ((), ())), preferred_element_type=F32)


def tn(a, b):
    return lax.dot_general(a, b, (((0,), (0,)), ((), ())), preferred_element_type=F32)


class Place:
    def __init__(self, tensor, dp):
        self.tensor = tensor
        self.groups = dp // CORES
        self.chips = tensor * self.groups
        self.pipe = lax.axis_index("pipe")
        self.d = lax.axis_index("dp")
        self.t = lax.axis_index("tensor")
        self.core = lax.rem(self.d, CORES)
        self.group = self.d // CORES
        odd = lax.rem(self.group, 2)
        self.ring = self.group * tensor + self.t + odd * (tensor - 1 - 2 * self.t)

    def at(self, ring):
        group = ring // self.tensor
        along = lax.rem(ring, self.tensor)
        odd = lax.rem(group, 2)
        return group, along + odd * (self.tensor - 1 - 2 * along)

    def neighbour(self, step):
        group, t = self.at(lax.rem(self.ring + step + self.chips, self.chips))
        return {"dp": group * CORES + self.core, "tensor": t}

    def sibling(self):
        return {"dp": self.group * CORES + 1 - self.core}


def meet(devices):
    barrier = pltpu.get_barrier_semaphore()
    for device in devices:
        pl.semaphore_signal(barrier, inc=1, device_id=device, device_id_type=MESH)
    pl.semaphore_wait(barrier, len(devices))


def halves(rows, columns):
    if rows % 32 == 0:
        return [(pl.ds(k * (rows // 2), rows // 2), pl.ds(0, columns)) for k in range(2)]
    cut = columns // LANES // 2 * LANES
    return [(pl.ds(0, rows), pl.ds(0, cut)), (pl.ds(0, rows), pl.ds(cut, columns - cut))]


def gather_kernel(
    tensor, dp, rows_ref, pack_ref, length_ref, table_ref, x_ref, w_ref, lengths_ref, tables_ref,
    local_sem, block_send, block_recv, pass_send, pass_recv, small_send, small_recv,
    ring_send, ring_recv, core_send, core_recv,
):
    here = Place(tensor, dp)
    c, t, chips = here.core, here.t, here.chips
    nrow = rows_ref.shape[0]
    sibling = here.sibling()
    to_right, to_left = here.neighbour(1), here.neighbour(-1)
    others = [{"tensor": lax.rem(t + k, tensor)} for k in range(1, tensor)]
    meet([to_right, to_left, sibling] + others)

    lengths = pltpu.make_async_remote_copy(
        length_ref, lengths_ref.at[c], small_send.at[0], small_recv.at[0], device_id=sibling, device_id_type=MESH
    )
    lengths.start()
    own_lengths = pltpu.make_async_copy(length_ref, lengths_ref.at[c], local_sem.at[0])
    own_lengths.start()
    own_table = pltpu.make_async_copy(table_ref, tables_ref.at[t], local_sem.at[1])
    own_table.start()
    tables = []
    for k in range(1, tensor):
        tables.append(
            pltpu.make_async_remote_copy(
                table_ref, tables_ref.at[t], small_send.at[k], small_recv.at[k], device_id=others[k - 1], device_id_type=MESH
            )
        )
        tables[-1].start()

    def to_chip(i):
        return pltpu.make_async_remote_copy(
            rows_ref.at[i], x_ref.at[:, t], block_send.at[i], block_recv.at[t],
            device_id={"tensor": nrow * c + i}, device_id_type=MESH,
        )

    def kept(i):
        return pltpu.make_async_copy(rows_ref.at[i], x_ref.at[:, t], local_sem.at[2])

    def kept_pass(i):
        return pltpu.make_async_remote_copy(
            rows_ref.at[i], x_ref.at[:, t], pass_send.at[t], pass_recv.at[t], device_id=sibling, device_id_type=MESH
        )

    def passed(s):
        return pltpu.make_async_remote_copy(
            x_ref.at[:, s], x_ref.at[:, s], pass_send.at[s], pass_recv.at[s], device_id=sibling, device_id_type=MESH
        )

    for i in range(nrow):
        mine = nrow * c + i == t

        @pl.when(mine)
        def _():
            kept(i).start()
            kept_pass(i).start()

        @pl.when(jnp.logical_not(mine))
        def _():
            to_chip(i).start()

    parts = halves(*pack_ref.shape)
    own_pack = pltpu.make_async_copy(pack_ref, w_ref.at[t, here.d], local_sem.at[3])
    own_pack.start()

    def shard(ring, part):
        group, at = here.at(ring)
        return w_ref.at[at, group * CORES + c, parts[part][0], parts[part][1]]

    def source(step, part):
        return lax.rem(here.ring + (1 if part else -1) * step + chips, chips)

    def onward(step, part, first=False):
        slot = shard(source(step, part), part)
        return pltpu.make_async_remote_copy(
            pack_ref.at[parts[part][0], parts[part][1]] if first else slot, slot,
            ring_send.at[part, step], ring_recv.at[part, step],
            device_id=to_left if part else to_right, device_id_type=MESH,
        )

    def across(step, part, first=False):
        slot = shard(source(step, part), part)
        return pltpu.make_async_remote_copy(
            pack_ref.at[parts[part][0], parts[part][1]] if first else slot, slot,
            core_send.at[part, step], core_recv.at[part, step], device_id=sibling, device_id_type=MESH,
        )

    for part in range(2):
        onward(0, part, True).start()
        across(0, part, True).start()

    takes = t // nrow == c
    for s in range(tensor):

        @pl.when(jnp.logical_and(takes, s != t))
        def _():
            pltpu.make_async_remote_copy(
                rows_ref.at[0], x_ref.at[:, s], block_send.at[0], block_recv.at[s], device_id=sibling, device_id_type=MESH
            ).wait_recv()
            passed(s).start()

    @pl.loop(1, chips)
    def _(step):
        for part in range(2):
            onward(step - 1, part).wait_recv()

            @pl.when(step < chips - 1)
            def _():
                onward(step, part).start()

            across(step, part).start()

    @pl.loop(0, chips)
    def _(step):
        for part in range(2):

            @pl.when(step < chips - 1)
            def _():
                onward(step, part).wait_send()

            across(step, part).wait_send()
            across(step, part).wait_recv()

    for i in range(nrow):
        mine = nrow * c + i == t

        @pl.when(mine)
        def _():
            kept(i).wait()
            kept_pass(i).wait_send()

        @pl.when(jnp.logical_not(mine))
        def _():
            to_chip(i).wait_send()

    for s in range(tensor):

        @pl.when(jnp.logical_and(takes, s != t))
        def _():
            passed(s).wait_send()

        @pl.when(jnp.logical_not(takes))
        def _():
            passed(s).wait_recv()

    lengths.wait()
    own_lengths.wait()
    own_table.wait()
    own_pack.wait()
    for table in tables:
        table.wait()


def gather(tensor, dp, rows, pack, lengths, table):
    chips = tensor * dp // CORES
    nrow, two, places, width = rows.shape
    sems = pltpu.SemaphoreType.DMA
    return pl.pallas_call(
        functools.partial(gather_kernel, tensor, dp),
        out_shape=(
            jax.ShapeDtypeStruct((two, tensor, places, width), rows.dtype),
            jax.ShapeDtypeStruct((tensor, dp) + pack.shape, pack.dtype),
            jax.ShapeDtypeStruct((CORES,) + lengths.shape, lengths.dtype),
            jax.ShapeDtypeStruct((tensor,) + table.shape, table.dtype),
        ),
        in_specs=[ANY] * 4,
        out_specs=(ANY,) * 4,
        scratch_shapes=[
            sems((4,)), sems((nrow,)), sems((tensor,)), sems((tensor,)), sems((tensor,)), sems((tensor,)), sems((tensor,)),
            sems((2, chips)), sems((2, chips)), sems((2, chips)), sems((2, chips)),
        ],
        compiler_params=pltpu.CompilerParams(collective_id=0, has_side_effects=True),
        name="gather",
    )(rows, pack, lengths, table)


def scatter_kernel(
    tensor, dp, grads_ref, small_ref, rows_ref, out_ref, small_out, rows_out,
    own, theirs, taken, small_own, small_theirs, small_taken, total,
    own_sem, core_send, core_recv, ring_send, ring_recv,
    sown_sem, score_send, score_recv, sring_send, sring_recv, block_send, block_recv, local_sem,
):
    here = Place(tensor, dp)
    c, t, chips = here.core, here.t, here.chips
    nrow = rows_out.shape[0]
    sibling = here.sibling()
    to_right, to_left = here.neighbour(1), here.neighbour(-1)
    line = [
        {"dp": here.group * CORES + lax.rem(c + j, CORES), "tensor": lax.rem(t + k, tensor)}
        for j in range(CORES)
        for k in range(tensor)
        if j + k > 0
    ]
    meet([to_right, to_left] + line)

    half = tensor // 2
    owner = t // nrow

    def block(k):
        place = here.pipe * (c * half + k % half) + (1 - here.pipe) * k
        which = here.pipe * (k // half) + (1 - here.pipe) * c
        return place, which

    def home(k):
        place, which = block(k)
        slot = rows_out.at[lax.rem(t, nrow), which]
        recv = block_recv.at[lax.rem(t, nrow), which]
        return (
            jnp.logical_and(place == t, owner == c),
            lambda: pltpu.make_async_copy(rows_ref.at[k], slot, recv),
            lambda: pltpu.make_async_remote_copy(
                rows_ref.at[k], slot, block_send.at[k], recv,
                device_id={"dp": here.group * CORES + owner, "tensor": place}, device_id_type=MESH,
            ),
        )

    for k in range(tensor):
        stays, inside, away = home(k)

        @pl.when(stays)
        def _():
            inside().start()

        @pl.when(jnp.logical_not(stays))
        def _():
            away().start()

    def across(ring):
        group, at = here.at(ring)
        return (
            pltpu.make_async_remote_copy(
                grads_ref.at[at, group * CORES + 1 - c], theirs.at[ring], core_send.at[ring], core_recv.at[ring],
                device_id=sibling, device_id_type=MESH,
            ),
            pltpu.make_async_remote_copy(
                small_ref.at[at, group * CORES + 1 - c], small_theirs.at[ring], score_send.at[ring], score_recv.at[ring],
                device_id=sibling, device_id_type=MESH,
            ),
        )

    def fetch(ring):
        group, at = here.at(ring)
        return (
            pltpu.make_async_copy(grads_ref.at[at, group * CORES + c], own.at[ring], own_sem.at[ring]),
            pltpu.make_async_copy(small_ref.at[at, group * CORES + c], small_own.at[ring], sown_sem.at[ring]),
        )

    def behind(step):
        return lax.rem(here.ring - step + chips, chips)

    def order(k):
        off = (2 * lax.rem(k, 2) - 1) * (k // 2 + 1) * (1 - k // (chips - 1))
        return lax.rem(here.ring + chips + off, chips)

    @pl.loop(0, chips)
    def _(k):
        for copy in across(order(k)) + fetch(order(k)):
            copy.start()

    rows, columns = out_ref.shape
    parts = halves(rows, columns)

    def add(ring, part, step, last):
        height = parts[part][0].size
        piece = 16 if height % 16 == 0 else height

        @pl.loop(0, height // piece)
        def _(k):
            at = pl.ds(pl.multiple_of(parts[part][0].start + k * piece, 8), piece)
            where = (at, parts[part][1])
            value = own[(ring,) + where].astype(F32) + theirs[(ring,) + where].astype(F32)
            if step is not None:
                value = value + taken[(step,) + where].astype(F32)
            if last:
                total[where] = value
            else:
                own[(ring,) + where] = value.astype(BF16)

    def onward(ring, step, part):
        where = (parts[part][0], parts[part][1])
        return pltpu.make_async_remote_copy(
            own.at[(ring,) + where], taken.at[(step,) + where], ring_send.at[part, step], ring_recv.at[part, step],
            device_id=to_left if part else to_right, device_id_type=MESH,
        )

    def small_onward(ring, step):
        return pltpu.make_async_remote_copy(
            small_own.at[ring], small_taken.at[step], sring_send.at[step], sring_recv.at[step],
            device_id=to_right, device_id_type=MESH,
        )

    def ready(ring):
        for copy in across(ring):
            copy.wait_recv()
        for copy in fetch(ring):
            copy.wait()

    def ahead(step):
        return lax.rem(here.ring + step, chips)

    half_chips = chips // 2

    @pl.loop(0, chips - 1)
    def _(step):
        right, left = behind(step + 1), ahead(step + 1)

        @pl.when(step < half_chips)
        def _():
            ready(right)

        @pl.when(step < chips - 1 - half_chips)
        def _():
            ready(left)

        @pl.when(step == 0)
        def _():
            add(right, 0, None, False)
            add(left, 1, None, False)
            small_own[right] = small_own[right] + small_theirs[right]

        @pl.when(step > 0)
        def _():
            onward(right, step - 1, 0).wait_recv()
            add(right, 0, step - 1, False)
            onward(right, step, 0).start()
            onward(left, step - 1, 1).wait_recv()
            add(left, 1, step - 1, False)
            onward(left, step, 1).start()
            small_onward(right, step - 1).wait_recv()
            small_own[right] = small_own[right] + small_theirs[right] + small_taken[step - 1]
            small_onward(right, step).start()

        @pl.when(step == 0)
        def _():
            onward(right, 0, 0).start()
            onward(left, 0, 1).start()
            small_onward(right, 0).start()

    ready(here.ring)
    for part in range(2):
        onward(here.ring, chips - 2, part).wait_recv()
        add(here.ring, part, chips - 2, True)
    small_onward(here.ring, chips - 2).wait_recv()
    small_out[...] = small_own[here.ring] + small_theirs[here.ring] + small_taken[chips - 2]
    finish = pltpu.make_async_copy(total, out_ref, local_sem.at[0])
    finish.start()

    @pl.loop(0, chips)
    def _(step):
        @pl.when(step < chips - 1)
        def _():
            onward(behind(step + 1), step, 0).wait_send()
            onward(ahead(step + 1), step, 1).wait_send()
            small_onward(behind(step + 1), step).wait_send()

        for copy in across(step):
            copy.wait_send()

    for k in range(tensor):
        stays, inside, away = home(k)

        @pl.when(jnp.logical_not(stays))
        def _():
            away().wait_send()

    for i in range(nrow):
        for which in range(2):
            pltpu.make_async_copy(rows_ref.at[0], rows_out.at[i, which], block_recv.at[i, which]).wait()
    finish.wait()


def scatter(tensor, dp, grads, small, rows, nrow):
    chips = tensor * dp // CORES
    shard = grads.shape[2:]
    tiny = small.shape[2:]
    sems = pltpu.SemaphoreType.DMA
    return pl.pallas_call(
        functools.partial(scatter_kernel, tensor, dp),
        out_shape=(
            jax.ShapeDtypeStruct(shard, F32),
            jax.ShapeDtypeStruct(tiny, F32),
            jax.ShapeDtypeStruct((nrow, 2) + rows.shape[1:], rows.dtype),
        ),
        in_specs=[ANY] * 3,
        out_specs=(ANY, VMEM, ANY),
        scratch_shapes=[
            pltpu.VMEM((chips,) + shard, BF16),
            pltpu.VMEM((chips,) + shard, BF16),
            pltpu.VMEM((chips - 1,) + shard, BF16),
            pltpu.VMEM((chips,) + tiny, F32),
            pltpu.VMEM((chips,) + tiny, F32),
            pltpu.VMEM((chips - 1,) + tiny, F32),
            pltpu.VMEM(shard, F32),
            sems((chips,)), sems((chips,)), sems((chips,)), sems((2, chips)), sems((2, chips)),
            sems((chips,)), sems((chips,)), sems((chips,)), sems((chips,)), sems((chips,)),
            sems((tensor,)), sems((nrow, 2)), sems((1,)),
        ],
        compiler_params=pltpu.CompilerParams(collective_id=1, has_side_effects=True, vmem_limit_bytes=VMEM_LIMIT),
        name="scatter",
    )(grads, small, rows)


KEY, VALUE, QUERY, OUT, FIRST, SECOND = range(6)


def rms(value):
    return lax.rsqrt(jnp.mean(value * value, axis=-1, keepdims=True) + EPSILON)


def in_rows(count, piece, body):
    @pl.loop(0, count // piece)
    def _(k):
        body(pl.ds(pl.multiple_of(k * piece, piece), piece))


def columns_of(count, body, piece=256):
    @pl.loop(0, count // piece)
    def _(k):
        body(pl.ds(pl.multiple_of(k * piece, piece), piece))


def normalize(source, gain, target, count):
    def body(at):
        value = source[at, :].astype(F32)
        target[at, :] = (value * rms(value) * gain).astype(BF16)

    in_rows(count, 32, body)


def normalize_back(source, gain, incoming, total, gain_out, count, fresh):
    gain_out[...] = jnp.zeros_like(gain_out)

    def body(at):
        value, back = source[at, :].astype(F32), incoming[at, :]
        scale = rms(value)
        unit = value * scale
        gain_out[...] += jnp.sum((back * unit).reshape(-1, 8, back.shape[-1]), axis=0)
        back = back * gain
        back = scale * (back - unit * jnp.mean(back * unit, axis=-1, keepdims=True))
        total[at, :] = back if fresh else total[at, :] + back

    in_rows(count, 32, body)


def project(left, weight, target, count):
    def body(at):
        target[0:count, at] = nn(left[0:count, :], weight[:, at]).astype(target.dtype)

    columns_of(weight.shape[1], body)


def project_back(left, weight, total, count, fresh):
    def body(at):
        value = nt(left[0:count, :], weight[at, :])
        total[0:count, at] = value if fresh else total[0:count, at] + value

    columns_of(weight.shape[0], body)


def lane_half(shape, part):
    return lax.broadcasted_iota(jnp.int32, shape, 1) // HEAD_DIM == part


def attend(keys, values, queries, mixture, probs, rows, span, pairs, mask, bias):
    @pl.loop(0, pairs)
    def _(pair):
        lanes = pl.ds(pl.multiple_of(pair * LANES, LANES), LANES)
        key, query = keys[0:span, lanes], queries[0:rows, lanes]
        value_t = values[0:span, lanes].T
        mixed = []
        for part in range(2):
            one = jnp.where(lane_half(query.shape, part), query, jnp.zeros_like(query))
            scores = nt(key, one) + mask[0:span, 0:rows]
            if bias is not None:
                scores = scores + bias(2 * pair + part)
            scores = jnp.exp(scores - jnp.max(scores, axis=0, keepdims=True))
            scores = (scores * (1.0 / jnp.sum(scores, axis=0, keepdims=True))).astype(BF16)
            probs[2 * pair + part, 0:span, 0:rows] = scores
            mixed.append(nn(value_t[part * HEAD_DIM : (part + 1) * HEAD_DIM, :], scores))
        mixture[0:rows, lanes] = jnp.concatenate(mixed, axis=0).T.astype(BF16)


def attend_back(keys, values, queries, back, probs, d_keys, d_values, d_queries, rows, span, pairs, each):
    @pl.loop(0, pairs)
    def _(pair):
        lanes = pl.ds(pl.multiple_of(pair * LANES, LANES), LANES)
        key, value = keys[0:span, lanes], values[0:span, lanes]
        query, given = queries[0:rows, lanes], back[0:rows, lanes]
        key_t = key.T
        d_key, d_value, d_query = None, None, []
        for part in range(2):
            side = lane_half(query.shape, part)
            query_one = jnp.where(side, query, jnp.zeros_like(query))
            given_one = jnp.where(side, given, jnp.zeros_like(given))
            prob = probs[2 * pair + part, 0:span, 0:rows]
            wide = prob.astype(F32)
            d_prob = nt(value, given_one)
            d_score = (wide * (d_prob - jnp.sum(wide * d_prob, axis=0, keepdims=True))).astype(BF16)
            if each is not None:
                each(2 * pair + part, d_score)
            of_key, of_value = nn(d_score, query_one), nn(prob, given_one)
            d_key = of_key if d_key is None else d_key + of_key
            d_value = of_value if d_value is None else d_value + of_value
            d_query.append(nn(key_t[part * HEAD_DIM : (part + 1) * HEAD_DIM, :], d_score))
        d_keys[0:span, lanes] = d_key.astype(BF16)
        d_values[0:span, lanes] = d_value.astype(BF16)
        d_queries[0:rows, lanes] = jnp.concatenate(d_query, axis=0).T.astype(BF16)


def segments(lengths_row, shape, axis, first):
    lane = lax.broadcasted_iota(jnp.int32, lengths_row.shape, 1)
    places = lax.broadcasted_iota(jnp.int32, shape, axis) + first
    ids = jnp.zeros(shape, jnp.int32)
    for c in range(SEGS_HELD):
        bound = jnp.sum(jnp.where(lane <= c, lengths_row, 0), axis=1, keepdims=True)
        ids = ids + (places >= bound).astype(jnp.int32)
    return ids


SEGS_HELD = 6


def block_kernel(
    tensor, dp, heads_at, x_ref, w_hbm, gain_ref, length_ref, table_ref, bucket_ref,
    grads_hbm, rows_out, gains_out, bias_out,
    raw, square, inner, outer, hidden, keys, values, queries, probs, mask, cross_mask, mixture,
    resid_mid, resid_top, d_resid, summed, second, third, slope, active, d_active, d_branch, branch,
    cross_keys, cross_values, cross_queries, cross_mixture, cross_probs, cross_back, cross_in, cross_in_back,
    d_cross_keys, d_cross_values, d_cross_queries, cross_taken, send_pair, send_back, joined,
    d_keys, d_values, d_queries, taken_pair, d_pair, turned, stage, vectors, diagonals, onehot, gain_parts,
    load_sem, stage_sem, send_sem, recv_sem,
):
    here = Place(tensor, dp)
    c, t = here.core, here.t
    width = x_ref.shape[1]
    tall = x_ref.shape[0]
    block = width // tensor
    half_width = width // 2
    sibling = here.sibling()
    across = [{"pipe": 1 - here.pipe, "dp": here.group * CORES + k} for k in range(CORES)]
    meet([sibling] + across)

    def loads(tt):
        return [
            pltpu.make_async_copy(w_hbm.at[tt, :, pl.ds(0, 6 * block)], raw.at[tt], load_sem.at[0, tt]),
            pltpu.make_async_copy(w_hbm.at[tt, :, pl.ds(6 * block, inner.shape[2])], inner.at[tt], load_sem.at[1, tt]),
            pltpu.make_async_copy(
                w_hbm.at[tt, :, pl.ds(6 * block + inner.shape[2], outer.shape[2])], outer.at[tt], load_sem.at[2, tt]
            ),
        ]

    for tt in range(tensor):
        loads(tt)[0].start()
    for tt in range(tensor):
        loads(tt)[1].start()
        loads(tt)[2].start()

    def move(source, target, sends, recvs, device):
        return pltpu.make_async_remote_copy(
            source, target, send_sem.at[sends], recv_sem.at[recvs], device_id=device, device_id_type=MESH
        )

    places = onehot.shape[1]
    buckets = lax.broadcasted_iota(jnp.int32, onehot.shape, 0) == bucket_ref[0:1, :]
    onehot[...] = buckets.astype(F32)
    for tt in range(tensor):
        vectors[pl.ds(8 * tt, 8), :] = lax.dot_general(
            table_ref[tt], onehot[...], (((1,), (0,)), ((), ())), precision=lax.Precision.HIGHEST, preferred_element_type=F32
        )
    nrow = tensor // CORES
    enc_row = length_ref[t // nrow, pl.ds(lax.rem(t, nrow), 1), :]
    dec_row = length_ref[t // nrow, pl.ds(nrow + lax.rem(t, nrow), 1), :]

    def masked(allowed):
        return jnp.where(allowed, 0.0, NEGATIVE).astype(F32)

    def vector_row(head):
        return (head // heads_at) * 8 + lax.rem(head, heads_at)

    def untangle():
        for tt in range(tensor):
            loads(tt)[0].wait()
            for k in range(6):
                square[k, :, tt * block : (tt + 1) * block] = raw[tt, :, k * block : (k + 1) * block]

    def self_forward(span, rows, first_row):
        def bias(head):
            pieces = []
            for j in range(span // LANES):
                start = pl.multiple_of(first_row + span - LANES - j * LANES, LANES)
                row = vectors[pl.ds(vector_row(head), 1), pl.ds(start, rows + LANES)]
                wide = jnp.broadcast_to(row, (LANES, rows + LANES))
                pieces.append(pltpu.roll(wide, rows + 1, 1, stride=1, stride_axis=0)[:, 0:rows])
            return jnp.concatenate(pieces, axis=0)

        normalize(x_ref, gain_ref[0:1, :], hidden, span)
        project(hidden, square.at[KEY], keys, span)
        project(hidden, square.at[VALUE], values, span)
        own = hidden.at[pl.ds(first_row, rows)]
        project(own, square.at[QUERY], queries, rows)
        attend(keys, values, queries, mixture, probs, rows, span, width // LANES, mask, bias)
        project_back(mixture, square.at[OUT], resid_mid, rows, True)

        def add(at):
            there = pl.ds(pl.multiple_of(first_row + at.start, 32), 32)
            resid_mid[at, :] += x_ref[there, :].astype(F32)

        in_rows(rows, 32, add)

    def feed_forward(rows):
        @pl.loop(0, tensor)
        def _(tt):
            def body(at):
                value = nn(second[0:rows, :], inner[tt, :, at])
                cdf = 0.5 * (1.0 + lax.erf(value * 0.7071067811865476))
                active[tt, 0:rows, at] = (value * cdf).astype(BF16)
                slope[tt, 0:rows, at] = cdf + value * jnp.exp(-0.5 * value * value) * 0.3989422804014327

            columns_of(inner.shape[2], body)

    def feed_out(target, rows):
        @pl.loop(0, tensor)
        def _(tt):
            def body(at):
                target[0:rows, at] += nt(active[tt, 0:rows, :], outer[tt, at, :])

            columns_of(width, body)

    def feed_back(rows, ready):
        summed[0:rows, :] = jnp.zeros((rows, width), F32)

        @pl.loop(0, tensor)
        def _(tt):
            def body(at):
                value = ready[tt, rows : 2 * rows, at] if ready is not None else nn(d_branch[0:rows, :], outer[tt, :, at])
                d_active[tt, 0:rows, at] = (value * slope[tt, 0:rows, at]).astype(BF16)

            columns_of(inner.shape[2], body)

            def back(at):
                summed[0:rows, at] += nt(d_active[tt, 0:rows, :], inner[tt, at, :])

            columns_of(width, back)

    def turn(left, rows):
        def body(at):
            turned[at, 0:rows] = left[0:rows, at].T

        columns_of(width, body, LANES)

    def feed_grads(rows, right, column):
        def out(tt, slot):
            return pltpu.make_async_copy(
                stage.at[slot], grads_hbm.at[tt, :, pl.ds(column, stage.shape[2])], stage_sem.at[slot]
            )

        @pl.loop(0, tensor)
        def _(tt):
            slot = lax.rem(tt, 2)

            @pl.when(tt >= 2)
            def _():
                out(tt, slot).wait()

            def body(at):
                stage[slot, :, at] = nn(turned[:, 0:rows], right[tt, 0:rows, at]).astype(BF16)

            columns_of(stage.shape[2], body)
            out(tt, slot).start()

        out(0, 0).wait()
        out(1, 1).wait()

    def square_grad(rows, right, which):
        for k in range(tensor // 2):
            value = nn(turned[:, 0:rows], right[0:rows, 2 * k * block : 2 * (k + 1) * block]).astype(BF16)
            raw[2 * k, :, which * block : (which + 1) * block] = value[:, 0:block]
            raw[2 * k + 1, :, which * block : (which + 1) * block] = value[:, block:]

    def to_bf16(source, target, rows):
        def body(at):
            target[at, :] = source[at, :].astype(BF16)

        in_rows(rows, 32, body)

    def gain_done(which):
        gains_out[which : which + 1, :] = jnp.sum(gain_parts[...], axis=0, keepdims=True)

    def self_backward(span, rows, first_row, mirror):
        to_bf16(d_resid, branch, rows)
        project(branch, square.at[OUT], d_branch, rows)
        diagonals[...] = jnp.zeros_like(diagonals)

        def each(head, d_score):
            for j in range(span // LANES):
                start = pl.multiple_of(first_row + span - LANES - j * LANES, LANES)
                piece = nn(mirror, d_score[j * LANES : (j + 1) * LANES, :])
                piece = jnp.concatenate([piece, jnp.zeros((LANES, LANES), F32)], axis=1)
                piece = pltpu.roll(piece, 0, 1, stride=1, stride_axis=0)
                at = (pl.ds(vector_row(head), 1), pl.ds(start, rows + LANES))
                diagonals[at] += jnp.sum(piece, axis=0, keepdims=True)

        attend_back(
            keys, values, queries, d_branch, probs, d_keys, d_values, d_queries, rows, span, width // LANES, each
        )
        far = pl.ds(pl.multiple_of((1 - c) * rows, rows), rows)
        near = pl.ds(pl.multiple_of(c * rows, rows), rows)
        trades = [
            move(source.at[far], taken_pair.at[k, pl.ds(0, rows)], 12 + k, 12 + k, sibling)
            for k, source in enumerate((d_keys, d_values))
        ]
        for trade in trades:
            trade.start()
        turn(branch, rows)
        square_grad(rows, mixture, OUT)
        for tt in range(tensor):
            bias_out[pl.ds(8 * tt, 8), :] = lax.dot_general(
                diagonals[pl.ds(8 * tt, 8), :], onehot[...], (((1,), (1,)), ((), ())),
                precision=lax.Precision.HIGHEST, preferred_element_type=F32,
            )
        for trade in trades:
            trade.wait_recv()
        for k, source in enumerate((d_keys, d_values)):
            d_pair[k, 0:rows, :] = (source[near, :].astype(F32) + taken_pair[k, 0:rows, :].astype(F32)).astype(BF16)
        project_back(d_queries, square.at[QUERY], summed, rows, True)
        project_back(d_pair.at[0], square.at[KEY], summed, rows, False)
        project_back(d_pair.at[1], square.at[VALUE], summed, rows, False)
        own = pl.ds(pl.multiple_of(first_row, rows), rows)
        normalize_back(x_ref.at[own], gain_ref[0:1, :], summed, d_resid, gain_parts, rows, False)
        gain_done(0)
        turn(hidden.at[own], rows)
        square_grad(rows, d_queries, QUERY)
        square_grad(rows, d_pair.at[0], KEY)
        square_grad(rows, d_pair.at[1], VALUE)
        for trade in trades:
            trade.wait_send()
        outs = [
            pltpu.make_async_copy(raw.at[tt], grads_hbm.at[tt, :, pl.ds(0, 6 * block)], load_sem.at[0, tt])
            for tt in range(tensor)
        ]
        for out in outs:
            out.start()
        for out in outs:
            out.wait()

    def wait_loads():
        for tt in range(tensor):
            loads(tt)[1].wait()
            loads(tt)[2].wait()

    mirror = (
        lax.broadcasted_iota(jnp.int32, (LANES, LANES), 0) + lax.broadcasted_iota(jnp.int32, (LANES, LANES), 1) == LANES - 1
    ).astype(BF16)
    gains_out[...] = jnp.zeros_like(gains_out)
    near_lanes = pl.ds(pl.multiple_of(c * half_width, half_width), half_width)
    far_lanes = pl.ds(pl.multiple_of((1 - c) * half_width, half_width), half_width)
    rows_e, span_e, rows_d, span_d = tall // 2, tall, tall // 4, tall // 2
    pairs_here = half_width // LANES

    def parts_of(array):
        return [array.at[pl.ds(k * rows_d, rows_d)] for k in range(CORES)]

    @pl.when(here.pipe == 0)
    def _():
        rows, span = rows_e, span_e
        first_row = pl.multiple_of(c * rows, rows)
        seg_rows = segments(enc_row, (span, 1), 0, 0)
        mask[...] = masked(seg_rows == segments(enc_row, (1, rows), 1, first_row))
        cross_mask[...] = masked(seg_rows == segments(dec_row, (1, span_d), 1, 0))
        untangle()
        self_forward(span, rows, first_row)
        wait_loads()
        normalize(resid_mid, gain_ref[1:2, :], second, rows)
        feed_forward(rows)
        resid_top[...] = resid_mid[...]
        feed_out(resid_top, rows)
        normalize(resid_top, gain_ref[2:3, :], third, rows)
        mine = pl.ds(first_row, rows)
        other = pl.ds(pl.multiple_of((1 - c) * rows, rows), rows)
        project(third, square.at[FIRST], d_pair.at[0], rows)
        project(third, square.at[SECOND], d_pair.at[1], rows)
        trades = []
        for k, held in enumerate((cross_keys, cross_values)):
            held[mine, :] = d_pair[k, :, near_lanes]
            send_pair[k] = d_pair[k, :, far_lanes]
            trades.append(move(send_pair.at[k], held.at[mine], k, k, sibling))
            trades[-1].start()
        for k, part in enumerate(parts_of(cross_queries)):
            move(part, part, 2 + k, 2 + k, across[k]).wait_recv()
        for k, held in enumerate((cross_keys, cross_values)):
            move(send_pair.at[k], held.at[other], k, k, sibling).wait_recv()
        attend(
            cross_keys, cross_values, cross_queries, cross_mixture, cross_probs, span_d, span, pairs_here, cross_mask, None
        )
        mixtures = [
            move(part, cross_in.at[c], 4 + k, 4 + c, across[k]) for k, part in enumerate(parts_of(cross_mixture))
        ]
        for mix in mixtures:
            mix.start()
        for k, part in enumerate(parts_of(cross_back)):
            move(part, part, 6 + k, 6 + k, across[k]).wait_recv()
        attend_back(
            cross_keys, cross_values, cross_queries, cross_back, cross_probs,
            d_cross_keys, d_cross_values, d_cross_queries, span_d, span, pairs_here, None,
        )
        returns = [
            move(d_cross.at[other], cross_taken.at[k], 10 + k, 10 + k, sibling)
            for k, d_cross in enumerate((d_cross_keys, d_cross_values))
        ]
        for back in returns:
            back.start()
        answers = [
            move(part, cross_in_back.at[c], 8 + k, 8 + c, across[k]) for k, part in enumerate(parts_of(d_cross_queries))
        ]
        for answer in answers:
            answer.start()
        for k, d_cross in enumerate((d_cross_keys, d_cross_values)):
            d_pair[k, :, near_lanes] = d_cross[mine, :]
            returns[k].wait_recv()
            d_pair[k, :, far_lanes] = cross_taken[k]
        project_back(d_pair.at[0], square.at[FIRST], summed, rows, True)
        project_back(d_pair.at[1], square.at[SECOND], summed, rows, False)
        normalize_back(resid_top, gain_ref[2:3, :], summed, d_resid, gain_parts, rows, True)
        gain_done(2)
        turn(third, rows)
        square_grad(rows, d_pair.at[0], FIRST)
        square_grad(rows, d_pair.at[1], SECOND)
        to_bf16(d_resid, d_branch, rows)
        feed_back(rows, None)
        normalize_back(resid_mid, gain_ref[1:2, :], summed, d_resid, gain_parts, rows, False)
        gain_done(1)
        turn(second, rows)
        feed_grads(rows, d_active, 6 * block)
        turn(d_branch, rows)
        feed_grads(rows, active, 6 * block + inner.shape[2])
        for copy in trades + mixtures + returns + answers:
            copy.wait_send()
        self_backward(span, rows, first_row, mirror)
        to_bf16(d_resid, rows_out, rows)

    @pl.when(here.pipe == 1)
    def _():
        rows, span = rows_d, span_d
        first_row = pl.multiple_of(c * rows, rows)
        key_at = lax.broadcasted_iota(jnp.int32, (span, rows), 0)
        query_at = lax.broadcasted_iota(jnp.int32, (span, rows), 1) + first_row
        same = segments(dec_row, (span, 1), 0, 0) == segments(dec_row, (1, rows), 1, first_row)
        mask[0:span, 0:rows] = masked(same & (query_at >= key_at))
        untangle()
        self_forward(span, rows, first_row)
        normalize(resid_mid, gain_ref[1:2, :], third, rows)
        project(third, square.at[FIRST], joined, rows)
        asks = []
        for k in range(CORES):
            send_pair[k, 0:rows, :] = joined[:, k * half_width : (k + 1) * half_width]
            asks.append(move(send_pair.at[k, pl.ds(0, rows)], parted(cross_queries, c, rows), 2 + k, 2 + c, across[k]))
            asks[-1].start()
        wait_loads()
        cotangent = pl.ds(pl.multiple_of(span + first_row, rows), rows)
        d_branch[0:rows, :] = x_ref[cotangent, :]

        @pl.loop(0, tensor)
        def _(tt):
            def body(at):
                slope[tt, rows : 2 * rows, at] = nn(d_branch[0:rows, :], outer[tt, :, at])

            columns_of(inner.shape[2], body)

        for k in range(CORES):
            move(cross_in.at[k], cross_in.at[k], 4 + k, 4 + k, across[k]).wait_recv()
            joined[:, k * half_width : (k + 1) * half_width] = cross_in[k]
        resid_top[0:rows, :] = resid_mid[0:rows, :]
        project_back(joined, square.at[SECOND], resid_top, rows, False)
        normalize(resid_top, gain_ref[2:3, :], second, rows)
        feed_forward(rows)
        feed_back(rows, slope)
        d_resid[0:rows, :] = d_branch[0:rows, :].astype(F32)
        normalize_back(resid_top, gain_ref[2:3, :], summed, d_resid, gain_parts, rows, False)
        gain_done(2)
        to_bf16(d_resid, branch, rows)
        project(branch, square.at[SECOND], d_queries, rows)
        tells = []
        for k in range(CORES):
            send_back[k] = d_queries[0:rows, k * half_width : (k + 1) * half_width]
            tells.append(move(send_back.at[k], parted(cross_back, c, rows), 6 + k, 6 + c, across[k]))
            tells[-1].start()
        feed_out(resid_top, rows)
        to_bf16(resid_top, rows_out, rows)
        turn(second, rows)
        feed_grads(rows, d_active, 6 * block)
        turn(d_branch, rows)
        feed_grads(rows, active, 6 * block + inner.shape[2])
        turn(branch, rows)
        square_grad(rows, joined, SECOND)
        for k in range(CORES):
            move(cross_in_back.at[k], cross_in_back.at[k], 8 + k, 8 + k, across[k]).wait_recv()
            joined[:, k * half_width : (k + 1) * half_width] = cross_in_back[k]
        project_back(joined, square.at[FIRST], summed, rows, True)
        normalize_back(resid_mid, gain_ref[1:2, :], summed, d_resid, gain_parts, rows, False)
        gain_done(1)
        turn(third, rows)
        square_grad(rows, joined, FIRST)
        for copy in asks + tells:
            copy.wait_send()
        self_backward(span, rows, first_row, mirror)
        to_bf16(d_resid, rows_out.at[pl.ds(rows, rows)], rows)


def parted(array, c, rows):
    return array.at[pl.ds(pl.multiple_of(c * rows, rows), rows)]


def blocks(tensor, dp, heads_at, rows, weights, gains, lengths, tables, buckets):
    tall, width = rows.shape
    block = width // tensor
    hidden_block = (weights.shape[2] - 6 * block) // 2
    half_rows, half_width = tall // 2, width // 2
    heads = heads_at * tensor
    ranges = buckets.shape[1]
    sems = pltpu.SemaphoreType.DMA

    def held(*shape, dtype=BF16):
        return pltpu.VMEM(shape, dtype)

    scratch = dict(
        raw=held(tensor, width, 6 * block),
        square=held(6, width, width),
        inner=held(tensor, width, hidden_block),
        outer=held(tensor, width, hidden_block),
        hidden=held(tall, width),
        keys=held(tall, width),
        values=held(tall, width),
        queries=held(half_rows, width),
        probs=held(heads, tall, half_rows),
        mask=held(tall, half_rows, dtype=F32),
        cross_mask=held(tall, half_rows, dtype=F32),
        mixture=held(half_rows, width),
        resid_mid=held(half_rows, width, dtype=F32),
        resid_top=held(half_rows, width, dtype=F32),
        d_resid=held(half_rows, width, dtype=F32),
        summed=held(half_rows, width, dtype=F32),
        second=held(half_rows, width),
        third=held(half_rows, width),
        slope=held(tensor, half_rows, hidden_block, dtype=F32),
        active=held(tensor, half_rows, hidden_block),
        d_active=held(tensor, half_rows, hidden_block),
        d_branch=held(half_rows, width),
        branch=held(half_rows, width),
        cross_keys=held(tall, half_width),
        cross_values=held(tall, half_width),
        cross_queries=held(half_rows, half_width),
        cross_mixture=held(half_rows, half_width),
        cross_probs=held(heads // CORES, tall, half_rows),
        cross_back=held(half_rows, half_width),
        cross_in=held(CORES, half_rows // 2, half_width),
        cross_in_back=held(CORES, half_rows // 2, half_width),
        d_cross_keys=held(tall, half_width),
        d_cross_values=held(tall, half_width),
        d_cross_queries=held(half_rows, half_width),
        cross_taken=held(CORES, half_rows, half_width),
        send_pair=held(CORES, half_rows, half_width),
        send_back=held(CORES, half_rows // 2, half_width),
        joined=held(half_rows // 2, width),
        d_keys=held(tall, width),
        d_values=held(tall, width),
        d_queries=held(half_rows, width),
        taken_pair=held(2, half_rows, width),
        d_pair=held(2, half_rows, width),
        turned=held(width, half_rows),
        stage=held(2, width, hidden_block),
        vectors=held(8 * tensor, ranges, dtype=F32),
        diagonals=held(8 * tensor, ranges, dtype=F32),
        onehot=held(LANES, ranges, dtype=F32),
        gain_parts=held(8, width, dtype=F32),
        load_sem=sems((3, tensor)),
        stage_sem=sems((2,)),
        send_sem=sems((14,)),
        recv_sem=sems((14,)),
    )
    return pl.pallas_call(
        functools.partial(block_kernel, tensor, dp, heads_at),
        out_shape=(
            jax.ShapeDtypeStruct(weights.shape, BF16),
            jax.ShapeDtypeStruct((half_rows, width), BF16),
            jax.ShapeDtypeStruct((8, width), F32),
            jax.ShapeDtypeStruct((8 * tensor, LANES), F32),
        ),
        in_specs=[VMEM, ANY] + [VMEM] * 4,
        out_specs=(ANY, VMEM, VMEM, VMEM),
        scratch_shapes=list(scratch.values()),
        compiler_params=pltpu.CompilerParams(collective_id=2, has_side_effects=True, vmem_limit_bytes=VMEM_LIMIT),
        name="blocks",
    )(rows, weights, gains, lengths, tables, buckets)


def pad_to(array, *shape):
    return jnp.pad(array, [(0, full - have) for full, have in zip(shape, array.shape)])


def shards(
    tensor, dp, section_rows, enc_lengths, dec_lengths, enc_buckets, dec_buckets, norm_gains, rel_bias,
    query_key_w, value_w, attn_out_w, cross_first, cross_second, ff_in, ff_out,
):
    nrow = section_rows.shape[1]
    depth, block = value_w.shape[1:]
    buckets, heads_at = rel_bias.shape[1:]
    on_encoder = lax.axis_index("pipe") == 0
    pack = jnp.concatenate(
        [query_key_w[0, 1], value_w[0], query_key_w[0, 0], attn_out_w[0].T, cross_first[0], cross_second[0], ff_in[0], ff_out[0].T],
        axis=1,
    )
    lengths = pad_to(jnp.concatenate([enc_lengths, dec_lengths], axis=0), 8, LANES)
    table = pad_to(rel_bias[0].T, 8, LANES)
    rows, weights, lengths, tables = gather(tensor, dp, section_rows[0], pack, lengths, table)
    ranges = -(-enc_buckets.shape[0] // LANES) * LANES
    dec_all = jnp.concatenate([jnp.zeros((dec_buckets.shape[0] - 1,), jnp.int32), dec_buckets])
    bucket_row = jnp.where(on_encoder, pad_to(enc_buckets, ranges), pad_to(dec_all, ranges))
    width = section_rows.shape[-1]
    grads, finished, gains, bias = blocks(
        tensor, dp, heads_at, rows.reshape(-1, width), weights.reshape(tensor, width, -1),
        pad_to(norm_gains[0], 8, width), lengths, tables, jnp.broadcast_to(bucket_row[None], (8, ranges)),
    )
    held = buckets // dp
    wide = -(-max(depth, held) // LANES) * LANES
    gain_part = pad_to(gains[:3].reshape(3, dp, depth).transpose(1, 0, 2), dp, 3, wide)
    bias_part = bias.reshape(tensor, 8, LANES)[:, :heads_at, :buckets].reshape(tensor, heads_at, dp, held)
    bias_part = pad_to(bias_part.transpose(0, 2, 1, 3), tensor, dp, 5, wide)
    small = jnp.concatenate([jnp.broadcast_to(gain_part[None], (tensor,) + gain_part.shape), bias_part], axis=2)
    total, tiny, home = scatter(
        tensor, dp, grads.reshape(tensor, dp, depth, -1), small, finished.reshape(tensor, -1, width), nrow
    )
    names = ("key", "value", "query", "out", "first", "second")
    part = {name: total[:, k * block : (k + 1) * block] for k, name in enumerate(names)}
    hidden_block = ff_in.shape[2]
    return (
        home.astype(F32)[None],
        tiny[:3, :depth][None],
        tiny[3 : 3 + heads_at, :held].T[None],
        jnp.stack([part["query"], part["key"]])[None],
        part["value"][None],
        part["out"].T[None],
        part["first"][None],
        part["second"][None],
        total[:, 6 * block : 6 * block + hidden_block][None],
        total[:, 6 * block + hidden_block :].T[None],
    )


def solution(mesh):
    sizes = dict(mesh.shape)
    return jax.shard_map(
        functools.partial(shards, sizes["tensor"], sizes["dp"]),
        mesh=mesh,
        in_specs=(
            P("pipe", "dp", None, "tensor", None),
            P("dp", None),
            P("dp", None),
            P(),
            P(),
            P("pipe", None, None),
            P("pipe", None, "tensor"),
            P("pipe", None, "dp", "tensor"),
            P("pipe", "dp", "tensor"),
            P("pipe", "tensor", "dp"),
            P("pipe", "dp", "tensor"),
            P("pipe", "dp", "tensor"),
            P("pipe", "dp", "tensor"),
            P("pipe", "tensor", "dp"),
        ),
        out_specs=(
            P("pipe", "dp", None, "tensor", None),
            P("pipe", None, "dp"),
            P("pipe", "dp", "tensor"),
            P("pipe", None, "dp", "tensor"),
            P("pipe", "dp", "tensor"),
            P("pipe", "tensor", "dp"),
            P("pipe", "dp", "tensor"),
            P("pipe", "dp", "tensor"),
            P("pipe", "dp", "tensor"),
            P("pipe", "tensor", "dp"),
        ),
        check_vma=False,
    )
```

time: 1470 us -> 331 us (0.23)
  blocking collectives: 465 us -> 0 us
  waiting for transfers between devices: 447 us -> 0 us
  Pallas kernels: 0 us -> 305 us
  matrix products: 193 us -> 0 us
  local copies, waits for them, and re-layouts: 185 us -> 17.5 us
  other arithmetic: 129 us -> 4.87 us
  between operations: 19.6 us -> 0.72 us
  starting transfers between devices: 17.1 us -> 0 us
    all_gather x27 -> x0, blocking collectives: 450 us -> none  [the longest x12 241 us: spread_rows(): return lax.all_gather(normed, 'tensor', axis=1, tiled=True)]
    reduce_scatter x30 -> x0, waiting for transfers between devices: 361 us -> none  [the longest x12 232 us: collect_grads(): lax.psum_scatter(partial_grads, 'tensor', scatter_dimension=1, tiled=True)]
    pallas_call x0 -> x3, Pallas kernels: none -> 305 us  [the longest x1 106 us: blocks(): pl.pallas_call(functools.partial(block_kernel, tensor, dp, heads_at), out...]
    dot_general x138 -> x0, matrix products: 193 us -> none  [the longest x4 21 us: feed_forward(): inner_sum = jnp.dot(hidden, w_inner, preferred_element_type=jnp.float32)]
    unnamed x534 -> x8, local copies, waits for them, and re-layouts: 105 us -> 4.32 us
    unnamed x48 -> x0, waiting for transfers between devices: 67.1 us -> none
    reduce_sum x33 -> x0, other arithmetic: 50.8 us -> none  [the longest x10 17.8 us: rms_norm(): inputs * lax.rsqrt(jnp.mean(inputs * inputs, axis=-1, keepdims=True) + EP...]
    reshape x6 -> x4, local copies, waits for them, and re-layouts: 36.4 us -> 0.2 us  [the longest x2 0.1 us: shards(): bias.reshape(tensor, 8, LANES)[:, :heads_at, :buckets]]
  transfers between devices with their start and end apart: 48 -> 0, of which waited for: 29 -> 0; matrix products, arithmetic and copies ran while one was open for 26% -> 0% of each run, Pallas kernels for 0% -> 0%
where the time goes in v1:
time: 331 us; the launch traced here: 329 us
  Pallas kernels  305 us (92%)
  local copies, waits for them, and re-layouts  17.5 us (5%)
  other arithmetic  4.87 us (1%)
    pallas_call x1, Pallas kernels, blocks(): pl.pallas_call(functools.partial(block_kernel, tensor, dp, heads_at), out...  106 us
    pallas_call x1, Pallas kernels, gather(): pl.pallas_call(functools.partial(gather_kernel, tensor, dp), out_shape=(j...  102 us
    pallas_call x1, Pallas kernels, scatter(): pl.pallas_call(functools.partial(scatter_kernel, tensor, dp), out_shape=(...  97.4 us

profile of v1, /device:TPU:8, one launch (start us, length us, event | category | flops | bytes accessed | tf_op | source)
XLA Modules:
  0.0 328.6 jit_solution(11101802367132840063)
XLA Ops:
  0.6 0.7 pad_add_fusion
  1.4 0.6 pad.29.length_ref
  2.0 0.7 copy.48
  2.6 0.6 pad.30.table_ref
  3.2 0.8 pad_select_fusion
  4.0 0.7 copy.47
  4.7 0.6 pad.31.gain_ref
  5.3 0.6 broadcast_in_dim.46.bucket_ref
  5.9 1.0 copy.29
  6.9 1.0 slice_bitcast_fusion.8
  7.9 3.2 concatenate.12.pack_ref
  11.1 101.9 %gather.1 = (bf16[2,4,64,768]{3,2,1,0:T(8,128)(2,1)}, bf16[4,4,192,2688]{3,2,1,0:T(8,128)(2,1)}, s32[2,8,128]{2,1,0:T(8,128)}, f32[4,8,128]{2,1,0:T(8,128)}) custom-call(bf16[2,2,64,768]{3,2,1,0:T(8,128)(2,1)} %bitcast.69, bf16[192,2688]{1,0:T(8,128)(2,1)} %concatenate.12.pack_ref, s32[8,128]{1,0:T(8,128)} %pad.29.length_ref, f32[8,128]{1,0:T(8,128)} %pad.30.table_ref), custom_call_target="tpu_custom_call" | custom-call | tf_op jit(solution)/shard_map/gather/pallas_call | solution.py:233
  113.0 106.2 %blocks.1 = (bf16[4,768,2688]{2,1,0:T(8,128)(2,1)}, bf16[256,768]{1,0:T(8,128)(2,1)}, f32[8,768]{1,0:T(8,128)}, f32[32,128]{1,0:T(8,128)}) custom-call(bf16[512,768]{1,0:T(8,128)(2,1)} %bitcast.67, bf16[4,768,2688]{2,1,0:T(8,128)(2,1)} %bitcast.65, f32[8,768]{1,0:T(8,128)} %pad.31.gain_ref, s32[2,8,128]{2,1,0:T(8,128)} %get-tuple-element.23.length_ref, ...), custom_call_target="tpu_custom_call" | custom-call | tf_op jit(solution)/shard_map/blocks/pallas_call | solution.py:1055
  219.3 0.7 slice.56
  220.0 0.7 slice.44
  220.7 0.1 reshape.46
  220.8 0.1 reshape.51
  221.0 0.7 select_maximum_fusion.small_ref
  221.6 97.4 %scatter.1 = (f32[192,2688]{1,0:T(8,128)}, f32[8,256]{1,0:T(8,128)}, bf16[2,2,64,768]{3,2,1,0:T(8,128)(2,1)}) custom-call(bf16[4,4,192,2688]{3,2,1,0:T(8,128)(2,1)} %bitcast.66, f32[4,4,8,256]{3,2,1,0:T(8,128)} %select_maximum_fusion.small_ref, bf16[4,64,768]{2,1,0:T(8,128)(2,1)} %bitcast.70), custom_call_target="tpu_custom_call" | custom-call | tf_op jit(solution)/shard_map/scatter/pallas_call | solution.py:452
  319.0 0.0 copy-start
  319.0 0.8 slice_bitcast_fusion.11
  319.9 0.7 slice_bitcast_fusion.10
  320.6 0.6 copy.33
  321.1 0.6 copy.34
  321.7 1.9 bitcast_convert_fusion
  323.6 2.3 slice_bitcast_fusion.2
  326.0 0.0 copy-done
  326.0 1.1 slice_bitcast_fusion
  327.1 0.8 copy.35
  327.9 0.8 maximum_bitcast_fusion
  (4 shorter events, 0.0 us)
Async XLA Ops:
  319.0 6.9 %copy-start = (f32[192,2688]{1,0:T(8,128)S(1)}, f32[192,2688]{1,0:T(8,128)}, u32[]{:S(2)}) copy-start(f32[192,2688]{1,0:T(8,128)} %get-tuple-element.31) | copy-start | bytes 6193156

commit v2 on v1

--- a/solution.py
+++ b/solution.py
@@ -1,4 +1,5 @@
 import functools
+import types
 
 import jax
 import jax.numpy as jnp
@@ -15,7 +16,7 @@
 HEAD_DIM = 64
 CORES = 2
 LANES = 128
-VMEM_LIMIT = 60 << 20
+VMEM_LIMIT = 62 << 20
 ANY = pl.BlockSpec(memory_space=pl.ANY)
 VMEM = pl.BlockSpec(memory_space=pltpu.VMEM)
 
@@ -476,13 +477,15 @@
 
 
 KEY, VALUE, QUERY, OUT, FIRST, SECOND = range(6)
+ATTN, CROSS, INNER, OUTER = range(4)
+SEGS_HELD = 6
 
 
 def rms(value):
     return lax.rsqrt(jnp.mean(value * value, axis=-1, keepdims=True) + EPSILON)
 
 
-def in_rows(count, piece, body):
+def in_rows(count, body, piece=32):
     @pl.loop(0, count // piece)
     def _(k):
         body(pl.ds(pl.multiple_of(k * piece, piece), piece))
@@ -491,7 +494,7 @@
 def columns_of(count, body, piece=256):
     @pl.loop(0, count // piece)
     def _(k):
-        body(pl.ds(pl.multiple_of(k * piece, piece), piece))
+        body(pl.ds(pl.multiple_of(k * piece, piece), piece), k)
 
 
 def normalize(source, gain, target, count):
@@ -499,44 +502,58 @@
         value = source[at, :].astype(F32)
         target[at, :] = (value * rms(value) * gain).astype(BF16)
 
-    in_rows(count, 32, body)
-
-
-def normalize_back(source, gain, incoming, total, gain_out, count, fresh):
-    gain_out[...] = jnp.zeros_like(gain_out)
+    in_rows(count, body)
+
+
+def normalize_back(source, gain, incoming, total, gain_parts, count, fresh):
+    gain_parts[...] = jnp.zeros_like(gain_parts)
 
     def body(at):
         value, back = source[at, :].astype(F32), incoming[at, :]
         scale = rms(value)
         unit = value * scale
-        gain_out[...] += jnp.sum((back * unit).reshape(-1, 8, back.shape[-1]), axis=0)
+        gain_parts[...] += jnp.sum((back * unit).reshape(-1, 8, back.shape[-1]), axis=0)
         back = back * gain
         back = scale * (back - unit * jnp.mean(back * unit, axis=-1, keepdims=True))
         total[at, :] = back if fresh else total[at, :] + back
 
-    in_rows(count, 32, body)
+    in_rows(count, body)
 
 
 def project(left, weight, target, count):
-    def body(at):
+    def body(at, k):
         target[0:count, at] = nn(left[0:count, :], weight[:, at]).astype(target.dtype)
 
     columns_of(weight.shape[1], body)
 
 
 def project_back(left, weight, total, count, fresh):
-    def body(at):
+    def body(at, k):
         value = nt(left[0:count, :], weight[at, :])
         total[0:count, at] = value if fresh else total[0:count, at] + value
 
     columns_of(weight.shape[0], body)
 
 
+def to_bf16(source, target, rows):
+    def body(at):
+        target[at, :] = source[at, :].astype(BF16)
+
+    in_rows(rows, body)
+
+
+def turn(left, turned, rows):
+    def body(at, k):
+        turned[at, 0:rows] = left[0:rows, at].T
+
+    columns_of(left.shape[1], body, LANES)
+
+
 def lane_half(shape, part):
     return lax.broadcasted_iota(jnp.int32, shape, 1) // HEAD_DIM == part
 
 
-def attend(keys, values, queries, mixture, probs, rows, span, pairs, mask, bias):
+def attend(keys, values, queries, mixture, probs, rows, span, pairs, mask, bias, after):
     @pl.loop(0, pairs)
     def _(pair):
         lanes = pl.ds(pl.multiple_of(pair * LANES, LANES), LANES)
@@ -553,9 +570,10 @@
             probs[2 * pair + part, 0:span, 0:rows] = scores
             mixed.append(nn(value_t[part * HEAD_DIM : (part + 1) * HEAD_DIM, :], scores))
         mixture[0:rows, lanes] = jnp.concatenate(mixed, axis=0).T.astype(BF16)
-
-
-def attend_back(keys, values, queries, back, probs, d_keys, d_values, d_queries, rows, span, pairs, each):
+        after(pair)
+
+
+def attend_back(keys, values, queries, back, probs, rows, span, pairs, each, after):
     @pl.loop(0, pairs)
     def _(pair):
         lanes = pl.ds(pl.multiple_of(pair * LANES, LANES), LANES)
@@ -577,9 +595,10 @@
             d_key = of_key if d_key is None else d_key + of_key
             d_value = of_value if d_value is None else d_value + of_value
             d_query.append(nn(key_t[part * HEAD_DIM : (part + 1) * HEAD_DIM, :], d_score))
-        d_keys[0:span, lanes] = d_key.astype(BF16)
-        d_values[0:span, lanes] = d_value.astype(BF16)
-        d_queries[0:rows, lanes] = jnp.concatenate(d_query, axis=0).T.astype(BF16)
+        keys[0:span, lanes] = d_key.astype(BF16)
+        values[0:span, lanes] = d_value.astype(BF16)
+        queries[0:rows, lanes] = jnp.concatenate(d_query, axis=0).T.astype(BF16)
+        after(pair)
 
 
 def segments(lengths_row, shape, axis, first):
@@ -592,179 +611,198 @@
     return ids
 
 
-SEGS_HELD = 6
-
-
-def block_kernel(
-    tensor, dp, heads_at, x_ref, w_hbm, gain_ref, length_ref, table_ref, bucket_ref,
-    grads_hbm, rows_out, gains_out, bias_out,
-    raw, square, inner, outer, hidden, keys, values, queries, probs, mask, cross_mask, mixture,
-    resid_mid, resid_top, d_resid, summed, second, third, slope, active, d_active, d_branch, branch,
-    cross_keys, cross_values, cross_queries, cross_mixture, cross_probs, cross_back, cross_in, cross_in_back,
-    d_cross_keys, d_cross_values, d_cross_queries, cross_taken, send_pair, send_back, joined,
-    d_keys, d_values, d_queries, taken_pair, d_pair, turned, stage, vectors, diagonals, onehot, gain_parts,
-    load_sem, stage_sem, send_sem, recv_sem,
-):
-    here = Place(tensor, dp)
+def masked(allowed):
+    return jnp.where(allowed, 0.0, NEGATIVE).astype(F32)
+
+
+def nothing(*unused):
+    pass
+
+
+def work(r, here, supply, drain, tensor, heads_at):
     c, t = here.core, here.t
-    width = x_ref.shape[1]
-    tall = x_ref.shape[0]
+    width = r.hidden.shape[1]
+    tall = r.hidden.shape[0]
     block = width // tensor
     half_width = width // 2
+    units = r.inner.shape[2]
+    places = r.x.shape[2]
     sibling = here.sibling()
     across = [{"pipe": 1 - here.pipe, "dp": here.group * CORES + k} for k in range(CORES)]
-    meet([sibling] + across)
-
-    def loads(tt):
-        return [
-            pltpu.make_async_copy(w_hbm.at[tt, :, pl.ds(0, 6 * block)], raw.at[tt], load_sem.at[0, tt]),
-            pltpu.make_async_copy(w_hbm.at[tt, :, pl.ds(6 * block, inner.shape[2])], inner.at[tt], load_sem.at[1, tt]),
-            pltpu.make_async_copy(
-                w_hbm.at[tt, :, pl.ds(6 * block + inner.shape[2], outer.shape[2])], outer.at[tt], load_sem.at[2, tt]
-            ),
-        ]
-
-    for tt in range(tensor):
-        loads(tt)[0].start()
-    for tt in range(tensor):
-        loads(tt)[1].start()
-        loads(tt)[2].start()
+    nrow = tensor // CORES
+    rows_e, span_e, rows_d, span_d = tall // 2, tall, tall // 4, tall // 2
+    pairs_here = half_width // LANES
+    near_lanes = pl.ds(pl.multiple_of(c * half_width, half_width), half_width)
+    far_lanes = pl.ds(pl.multiple_of((1 - c) * half_width, half_width), half_width)
+    lane_halves = [slice(k * half_width, (k + 1) * half_width) for k in range(CORES)]
 
     def move(source, target, sends, recvs, device):
         return pltpu.make_async_remote_copy(
-            source, target, send_sem.at[sends], recv_sem.at[recvs], device_id=device, device_id_type=MESH
-        )
-
-    places = onehot.shape[1]
-    buckets = lax.broadcasted_iota(jnp.int32, onehot.shape, 0) == bucket_ref[0:1, :]
-    onehot[...] = buckets.astype(F32)
-    for tt in range(tensor):
-        vectors[pl.ds(8 * tt, 8), :] = lax.dot_general(
-            table_ref[tt], onehot[...], (((1,), (0,)), ((), ())), precision=lax.Precision.HIGHEST, preferred_element_type=F32
-        )
-    nrow = tensor // CORES
-    enc_row = length_ref[t // nrow, pl.ds(lax.rem(t, nrow), 1), :]
-    dec_row = length_ref[t // nrow, pl.ds(nrow + lax.rem(t, nrow), 1), :]
-
-    def masked(allowed):
-        return jnp.where(allowed, 0.0, NEGATIVE).astype(F32)
+            source, target, r.send_sem.at[sends], r.recv_sem.at[recvs], device_id=device, device_id_type=MESH
+        )
+
+    def lengths_row(first):
+        return r.lengths[t // nrow, pl.ds(first + lax.rem(t, nrow), 1), :]
 
     def vector_row(head):
         return (head // heads_at) * 8 + lax.rem(head, heads_at)
 
-    def untangle():
+    def bias_vectors():
+        buckets = lax.broadcasted_iota(jnp.int32, r.onehot.shape, 0) == r.buckets[0:1, :]
+        r.onehot[...] = buckets.astype(F32)
         for tt in range(tensor):
-            loads(tt)[0].wait()
-            for k in range(6):
-                square[k, :, tt * block : (tt + 1) * block] = raw[tt, :, k * block : (k + 1) * block]
-
-    def self_forward(span, rows, first_row):
+            r.vectors[pl.ds(8 * tt, 8), :] = lax.dot_general(
+                r.tables[tt][:, 0 : r.onehot.shape[0]], r.onehot[...], (((1,), (0,)), ((), ())),
+                precision=lax.Precision.HIGHEST, preferred_element_type=F32,
+            )
+
+    def rows_ready(span, rows, first_block):
+        @pl.loop(0, span // places)
+        def _(k):
+            value = r.x[k // tensor, lax.rem(k, tensor)].astype(F32)
+            at = pl.ds(pl.multiple_of(k * places, places), places)
+            r.hidden[at, :] = (value * rms(value) * r.gains[0:1, :]).astype(BF16)
+
+        for k in range(rows // places):
+            r.own_x[k * places : (k + 1) * places, :] = r.x[first_block // tensor, lax.rem(first_block, tensor) + k]
+
+    def untangle(source, first, count):
+        for tt in range(tensor):
+            for k in range(count):
+                r.square[first + k, :, tt * block : (tt + 1) * block] = source[tt, :, k * block : (k + 1) * block]
+
+    def self_forward(span, rows, first_row, group, following):
         def bias(head):
             pieces = []
             for j in range(span // LANES):
                 start = pl.multiple_of(first_row + span - LANES - j * LANES, LANES)
-                row = vectors[pl.ds(vector_row(head), 1), pl.ds(start, rows + LANES)]
+                row = r.vectors[pl.ds(vector_row(head), 1), pl.ds(start, rows + LANES)]
                 wide = jnp.broadcast_to(row, (LANES, rows + LANES))
                 pieces.append(pltpu.roll(wide, rows + 1, 1, stride=1, stride_axis=0)[:, 0:rows])
             return jnp.concatenate(pieces, axis=0)
 
-        normalize(x_ref, gain_ref[0:1, :], hidden, span)
-        project(hidden, square.at[KEY], keys, span)
-        project(hidden, square.at[VALUE], values, span)
-        own = hidden.at[pl.ds(first_row, rows)]
-        project(own, square.at[QUERY], queries, rows)
-        attend(keys, values, queries, mixture, probs, rows, span, width // LANES, mask, bias)
-        project_back(mixture, square.at[OUT], resid_mid, rows, True)
+        untangle(r.raw_a, KEY, 2)
+        untangle(r.raw_a.at[:, :, pl.ds(2 * block, 2 * block)], QUERY, 2)
+        project(r.hidden, r.square.at[KEY], r.keys, span)
+        supply.tick(group, 0)
+        project(r.hidden, r.square.at[VALUE], r.values, span)
+        project(r.hidden.at[pl.ds(first_row, rows)], r.square.at[QUERY], r.queries, rows)
+        supply.tick(group, 1)
+
+        def after(pair):
+            @pl.when(pair < supply.count - 3)
+            def _():
+                supply.tick(group, 2 + pair)
+
+            if supply.count - 2 < 2 + width // LANES:
+
+                @pl.when(pair == supply.count - 4)
+                def _():
+                    supply.begin(following)
+
+        attend(r.keys, r.values, r.queries, r.mixture, r.probs, rows, span, width // LANES, r.mask, bias, after)
+        project_back(r.mixture, r.square.at[OUT], r.resid_mid, rows, True)
 
         def add(at):
-            there = pl.ds(pl.multiple_of(first_row + at.start, 32), 32)
-            resid_mid[at, :] += x_ref[there, :].astype(F32)
-
-        in_rows(rows, 32, add)
-
-    def feed_forward(rows):
+            r.resid_mid[at, :] += r.own_x[at, :].astype(F32)
+
+        in_rows(rows, add)
+        supply.ticks(group, supply.count - 1, supply.count)
+        supply.finish(group)
+
+    def every_other(group, n):
+        @pl.when(lax.rem(n, 2) == 1)
+        def _():
+            supply.tick(group, lax.div(n, 2))
+
+    def feed_forward(rows, group):
         @pl.loop(0, tensor)
         def _(tt):
-            def body(at):
-                value = nn(second[0:rows, :], inner[tt, :, at])
+            def body(at, k):
+                value = nn(r.second[0:rows, :], r.inner[tt, :, at])
                 cdf = 0.5 * (1.0 + lax.erf(value * 0.7071067811865476))
-                active[tt, 0:rows, at] = (value * cdf).astype(BF16)
-                slope[tt, 0:rows, at] = cdf + value * jnp.exp(-0.5 * value * value) * 0.3989422804014327
-
-            columns_of(inner.shape[2], body)
-
-    def feed_out(target, rows):
+                r.ff[tt, 0:rows, at] = (value * cdf).astype(BF16)
+                slope = cdf + value * jnp.exp(-0.5 * value * value) * 0.3989422804014327
+                r.ff[tensor + tt, 0:rows, at] = slope.astype(BF16)
+                if group is not None:
+                    every_other(group, tt * (units // 256) + k)
+
+            columns_of(units, body)
+
+    def feed_out(target, rows, group):
         @pl.loop(0, tensor)
         def _(tt):
-            def body(at):
-                target[0:rows, at] += nt(active[tt, 0:rows, :], outer[tt, at, :])
+            def body(at, k):
+                target[0:rows, at] += nt(r.ff[tt, 0:rows, :], r.outer[tt, at, :])
+                if group is not None:
+                    every_other(group, tt * (width // 256) + k)
 
             columns_of(width, body)
 
-    def feed_back(rows, ready):
-        summed[0:rows, :] = jnp.zeros((rows, width), F32)
+    def feed_back(rows, ready, group):
+        r.summed[0:rows, :] = jnp.zeros((rows, width), F32)
 
         @pl.loop(0, tensor)
         def _(tt):
-            def body(at):
-                value = ready[tt, rows : 2 * rows, at] if ready is not None else nn(d_branch[0:rows, :], outer[tt, :, at])
-                d_active[tt, 0:rows, at] = (value * slope[tt, 0:rows, at]).astype(BF16)
-
-            columns_of(inner.shape[2], body)
-
-            def back(at):
-                summed[0:rows, at] += nt(d_active[tt, 0:rows, :], inner[tt, at, :])
+            def body(at, k):
+                if ready:
+                    value = r.ff[tensor + tt, rows : 2 * rows, at].astype(F32)
+                else:
+                    value = nn(r.d_branch[0:rows, :], r.outer[tt, :, at])
+                r.ff[tensor + tt, 0:rows, at] = (value * r.ff[tensor + tt, 0:rows, at].astype(F32)).astype(BF16)
+
+            columns_of(units, body)
+
+            def back(at, k):
+                r.summed[0:rows, at] += nt(r.ff[tensor + tt, 0:rows, :], r.inner[tt, at, :])
 
             columns_of(width, back)
-
-    def turn(left, rows):
-        def body(at):
-            turned[at, 0:rows] = left[0:rows, at].T
-
-        columns_of(width, body, LANES)
-
-    def feed_grads(rows, right, column):
-        def out(tt, slot):
-            return pltpu.make_async_copy(
-                stage.at[slot], grads_hbm.at[tt, :, pl.ds(column, stage.shape[2])], stage_sem.at[slot]
-            )
-
+            if group is not None:
+                drain.tick(group, tt)
+
+    def feed_grads(rows, turned, first, which, hook):
         @pl.loop(0, tensor)
         def _(tt):
             slot = lax.rem(tt, 2)
 
             @pl.when(tt >= 2)
             def _():
-                out(tt, slot).wait()
-
-            def body(at):
-                stage[slot, :, at] = nn(turned[:, 0:rows], right[tt, 0:rows, at]).astype(BF16)
-
-            columns_of(stage.shape[2], body)
-            out(tt, slot).start()
-
-        out(0, 0).wait()
-        out(1, 1).wait()
-
-    def square_grad(rows, right, which):
+                drain.release(which, tt - 2, slot)
+
+            def body(at, k):
+                r.stage[slot, :, at] = nn(turned[:, 0:rows], r.ff[first + tt, 0:rows, at]).astype(BF16)
+                hook(tt, k)
+
+            columns_of(units, body)
+            drain.emit(which, tt, slot)
+
+        for tt in range(tensor - 2, tensor):
+            drain.release(which, tt, tt % 2)
+
+    def square_grads(rows, which, products, hook):
         for k in range(tensor // 2):
-            value = nn(turned[:, 0:rows], right[0:rows, 2 * k * block : 2 * (k + 1) * block]).astype(BF16)
-            raw[2 * k, :, which * block : (which + 1) * block] = value[:, 0:block]
-            raw[2 * k + 1, :, which * block : (which + 1) * block] = value[:, block:]
-
-    def to_bf16(source, target, rows):
-        def body(at):
-            target[at, :] = source[at, :].astype(BF16)
-
-        in_rows(rows, 32, body)
+            for j, (turned, right) in enumerate(products):
+                value = nn(turned[:, 0:rows], right[0:rows, 2 * k * block : 2 * (k + 1) * block]).astype(BF16)
+                for slot in range(2):
+                    r.stage[slot, :, j * block : (j + 1) * block] = value[:, slot * block : (slot + 1) * block]
+            for slot in range(2):
+                drain.emit(which, 2 * k + slot, slot)
+            hook(k)
+            for slot in range(2):
+                drain.release(which, 2 * k + slot, slot)
 
     def gain_done(which):
-        gains_out[which : which + 1, :] = jnp.sum(gain_parts[...], axis=0, keepdims=True)
-
-    def self_backward(span, rows, first_row, mirror):
-        to_bf16(d_resid, branch, rows)
-        project(branch, square.at[OUT], d_branch, rows)
-        diagonals[...] = jnp.zeros_like(diagonals)
+        r.gains_out[which : which + 1, :] = jnp.sum(r.gain_parts[...], axis=0, keepdims=True)
+
+    def self_backward(span, rows, first_row, group, send_rows):
+        mirror = (
+            lax.broadcasted_iota(jnp.int32, (LANES, LANES), 0) + lax.broadcasted_iota(jnp.int32, (LANES, LANES), 1)
+            == LANES - 1
+        ).astype(BF16)
+        to_bf16(r.d_resid, r.branch, rows)
+        project(r.branch, r.square.at[OUT], r.d_branch, rows)
+        drain.tick(group, 0)
+        r.diagonals[...] = jnp.zeros_like(r.diagonals)
 
         def each(head, d_score):
             for j in range(span // LANES):
@@ -773,145 +811,171 @@
                 piece = jnp.concatenate([piece, jnp.zeros((LANES, LANES), F32)], axis=1)
                 piece = pltpu.roll(piece, 0, 1, stride=1, stride_axis=0)
                 at = (pl.ds(vector_row(head), 1), pl.ds(start, rows + LANES))
-                diagonals[at] += jnp.sum(piece, axis=0, keepdims=True)
-
+                r.diagonals[at] += jnp.sum(piece, axis=0, keepdims=True)
+
+        pairs = width // LANES
         attend_back(
-            keys, values, queries, d_branch, probs, d_keys, d_values, d_queries, rows, span, width // LANES, each
+            r.keys, r.values, r.queries, r.d_branch, r.probs, rows, span, pairs, each,
+            lambda pair: drain.tick(group, 1 + lax.div(pair, pairs // 2), lax.rem(pair, pairs // 2) == 1),
         )
         far = pl.ds(pl.multiple_of((1 - c) * rows, rows), rows)
         near = pl.ds(pl.multiple_of(c * rows, rows), rows)
         trades = [
-            move(source.at[far], taken_pair.at[k, pl.ds(0, rows)], 12 + k, 12 + k, sibling)
-            for k, source in enumerate((d_keys, d_values))
+            move(source.at[far], r.taken_pair.at[k, pl.ds(0, rows)], 12 + k, 12 + k, sibling)
+            for k, source in enumerate((r.keys, r.values))
         ]
         for trade in trades:
             trade.start()
-        turn(branch, rows)
-        square_grad(rows, mixture, OUT)
+        turn(r.branch, r.turned, rows)
+        turn(r.hidden.at[pl.ds(first_row, rows)], r.turned_more, rows)
         for tt in range(tensor):
-            bias_out[pl.ds(8 * tt, 8), :] = lax.dot_general(
-                diagonals[pl.ds(8 * tt, 8), :], onehot[...], (((1,), (1,)), ((), ())),
+            at = pl.ds(8 * tt, 8)
+            r.bias_out[at, 0 : r.onehot.shape[0]] = lax.dot_general(
+                r.diagonals[at, :], r.onehot[...], (((1,), (1,)), ((), ())),
                 precision=lax.Precision.HIGHEST, preferred_element_type=F32,
             )
+        project_back(r.queries, r.square.at[QUERY], r.summed, rows, True)
         for trade in trades:
             trade.wait_recv()
-        for k, source in enumerate((d_keys, d_values)):
-            d_pair[k, 0:rows, :] = (source[near, :].astype(F32) + taken_pair[k, 0:rows, :].astype(F32)).astype(BF16)
-        project_back(d_queries, square.at[QUERY], summed, rows, True)
-        project_back(d_pair.at[0], square.at[KEY], summed, rows, False)
-        project_back(d_pair.at[1], square.at[VALUE], summed, rows, False)
-        own = pl.ds(pl.multiple_of(first_row, rows), rows)
-        normalize_back(x_ref.at[own], gain_ref[0:1, :], summed, d_resid, gain_parts, rows, False)
+        for k, source in enumerate((r.keys, r.values)):
+            r.d_pair[k, 0:rows, :] = (source[near, :].astype(F32) + r.taken_pair[k, 0:rows, :].astype(F32)).astype(BF16)
+        project_back(r.d_pair.at[0], r.square.at[KEY], r.summed, rows, False)
+        project_back(r.d_pair.at[1], r.square.at[VALUE], r.summed, rows, False)
+        drain.tick(group, 3)
+        normalize_back(r.own_x, r.gains[0:1, :], r.summed, r.d_resid, r.gain_parts, rows, False)
         gain_done(0)
-        turn(hidden.at[own], rows)
-        square_grad(rows, d_queries, QUERY)
-        square_grad(rows, d_pair.at[0], KEY)
-        square_grad(rows, d_pair.at[1], VALUE)
+        send_rows()
+        drain.small_begin()
+        products = [(r.turned_more, r.d_pair.at[0]), (r.turned_more, r.d_pair.at[1]), (r.turned_more, r.queries), (r.turned, r.mixture)]
+        square_grads(rows, ATTN, products, nothing)
         for trade in trades:
             trade.wait_send()
-        outs = [
-            pltpu.make_async_copy(raw.at[tt], grads_hbm.at[tt, :, pl.ds(0, 6 * block)], load_sem.at[0, tt])
-            for tt in range(tensor)
-        ]
-        for out in outs:
-            out.start()
-        for out in outs:
-            out.wait()
-
-    def wait_loads():
-        for tt in range(tensor):
-            loads(tt)[1].wait()
-            loads(tt)[2].wait()
-
-    mirror = (
-        lax.broadcasted_iota(jnp.int32, (LANES, LANES), 0) + lax.broadcasted_iota(jnp.int32, (LANES, LANES), 1) == LANES - 1
-    ).astype(BF16)
-    gains_out[...] = jnp.zeros_like(gains_out)
-    near_lanes = pl.ds(pl.multiple_of(c * half_width, half_width), half_width)
-    far_lanes = pl.ds(pl.multiple_of((1 - c) * half_width, half_width), half_width)
-    rows_e, span_e, rows_d, span_d = tall // 2, tall, tall // 4, tall // 2
-    pairs_here = half_width // LANES
+        drain.ticks(group, 4, drain.count)
+        drain.begin(ATTN)
+        drain.end(group)
+        drain.ticks(ATTN, 0, drain.count)
+        drain.end(ATTN)
 
     def parts_of(array):
         return [array.at[pl.ds(k * rows_d, rows_d)] for k in range(CORES)]
+
+    def part_here(array):
+        return array.at[pl.ds(pl.multiple_of(c * rows_d, rows_d), rows_d)]
+
+    r.gains_out[...] = jnp.zeros_like(r.gains_out)
+    r.bias_out[...] = jnp.zeros_like(r.bias_out)
+    supply.start()
+    supply.ticks(ATTN, 0, 2)
+    supply.small()
+    bias_vectors()
+    supply.rows()
 
     @pl.when(here.pipe == 0)
     def _():
         rows, span = rows_e, span_e
         first_row = pl.multiple_of(c * rows, rows)
-        seg_rows = segments(enc_row, (span, 1), 0, 0)
-        mask[...] = masked(seg_rows == segments(enc_row, (1, rows), 1, first_row))
-        cross_mask[...] = masked(seg_rows == segments(dec_row, (1, span_d), 1, 0))
-        untangle()
-        self_forward(span, rows, first_row)
-        wait_loads()
-        normalize(resid_mid, gain_ref[1:2, :], second, rows)
-        feed_forward(rows)
-        resid_top[...] = resid_mid[...]
-        feed_out(resid_top, rows)
-        normalize(resid_top, gain_ref[2:3, :], third, rows)
+        seg_rows = segments(lengths_row(0), (span, 1), 0, 0)
+        r.mask[...] = masked(seg_rows == segments(lengths_row(0), (1, rows), 1, first_row))
+        supply.ticks(ATTN, 2, 4)
+        rows_ready(span, rows, c * tensor)
+        supply.ticks(ATTN, 4, supply.count - 1)
+        supply.begin(INNER)
+        supply.ticks(ATTN, supply.count - 1, supply.count)
+        supply.finish(ATTN)
+        self_forward(span, rows, first_row, INNER, OUTER)
+        normalize(r.resid_mid, r.gains[1:2, :], r.second, rows)
+        feed_forward(rows, OUTER)
+        supply.begin(CROSS)
+        supply.ticks(OUTER, supply.count - 1, supply.count)
+        supply.finish(OUTER)
+        r.resid_top[...] = r.resid_mid[...]
+        feed_out(r.resid_top, rows, CROSS)
+        normalize(r.resid_top, r.gains[2:3, :], r.third, rows)
+        r.mask[...] = masked(seg_rows == segments(lengths_row(nrow), (1, span_d), 1, 0))
+        supply.ticks(CROSS, supply.count - 1, supply.count)
+        supply.finish(CROSS)
+        untangle(r.raw_c, FIRST, 2)
         mine = pl.ds(first_row, rows)
         other = pl.ds(pl.multiple_of((1 - c) * rows, rows), rows)
-        project(third, square.at[FIRST], d_pair.at[0], rows)
-        project(third, square.at[SECOND], d_pair.at[1], rows)
+        project(r.third, r.square.at[FIRST], r.d_pair.at[0], rows)
+        project(r.third, r.square.at[SECOND], r.d_pair.at[1], rows)
         trades = []
-        for k, held in enumerate((cross_keys, cross_values)):
-            held[mine, :] = d_pair[k, :, near_lanes]
-            send_pair[k] = d_pair[k, :, far_lanes]
-            trades.append(move(send_pair.at[k], held.at[mine], k, k, sibling))
+        for k, held in enumerate((r.cross_keys, r.cross_values)):
+            held[mine, :] = r.d_pair[k, :, near_lanes]
+            r.send_pair[k] = r.d_pair[k, :, far_lanes]
+            trades.append(move(r.send_pair.at[k], held.at[mine], k, k, sibling))
             trades[-1].start()
-        for k, part in enumerate(parts_of(cross_queries)):
+        for k, part in enumerate(parts_of(r.cross_queries)):
             move(part, part, 2 + k, 2 + k, across[k]).wait_recv()
-        for k, held in enumerate((cross_keys, cross_values)):
-            move(send_pair.at[k], held.at[other], k, k, sibling).wait_recv()
+        for k, held in enumerate((r.cross_keys, r.cross_values)):
+            move(r.send_pair.at[k], held.at[other], k, k, sibling).wait_recv()
         attend(
-            cross_keys, cross_values, cross_queries, cross_mixture, cross_probs, span_d, span, pairs_here, cross_mask, None
+            r.cross_keys, r.cross_values, r.cross_queries, r.cross_mixture, r.cross_probs, span_d, span, pairs_here,
+            r.mask, None, nothing,
         )
         mixtures = [
-            move(part, cross_in.at[c], 4 + k, 4 + c, across[k]) for k, part in enumerate(parts_of(cross_mixture))
+            move(part, r.cross_in.at[c], 4 + k, 4 + c, across[k]) for k, part in enumerate(parts_of(r.cross_mixture))
         ]
         for mix in mixtures:
             mix.start()
-        for k, part in enumerate(parts_of(cross_back)):
+        supply.close()
+        drain.free(0)
+        turn(r.third, r.turned, rows)
+        for k, part in enumerate(parts_of(r.cross_back)):
             move(part, part, 6 + k, 6 + k, across[k]).wait_recv()
         attend_back(
-            cross_keys, cross_values, cross_queries, cross_back, cross_probs,
-            d_cross_keys, d_cross_values, d_cross_queries, span_d, span, pairs_here, None,
+            r.cross_keys, r.cross_values, r.cross_queries, r.cross_back, r.cross_probs, span_d, span, pairs_here, None, nothing
         )
         returns = [
-            move(d_cross.at[other], cross_taken.at[k], 10 + k, 10 + k, sibling)
-            for k, d_cross in enumerate((d_cross_keys, d_cross_values))
+            move(d_cross.at[other], r.cross_taken.at[k], 10 + k, 10 + k, sibling)
+            for k, d_cross in enumerate((r.cross_keys, r.cross_values))
         ]
         for back in returns:
             back.start()
         answers = [
-            move(part, cross_in_back.at[c], 8 + k, 8 + c, across[k]) for k, part in enumerate(parts_of(d_cross_queries))
+            move(part, r.cross_in_back.at[c], 8 + k, 8 + c, across[k]) for k, part in enumerate(parts_of(r.cross_queries))
         ]
         for answer in answers:
             answer.start()
-        for k, d_cross in enumerate((d_cross_keys, d_cross_values)):
-            d_pair[k, :, near_lanes] = d_cross[mine, :]
+        for k, d_cross in enumerate((r.cross_keys, r.cross_values)):
+            r.d_pair[k, :, near_lanes] = d_cross[mine, :]
             returns[k].wait_recv()
-            d_pair[k, :, far_lanes] = cross_taken[k]
-        project_back(d_pair.at[0], square.at[FIRST], summed, rows, True)
-        project_back(d_pair.at[1], square.at[SECOND], summed, rows, False)
-        normalize_back(resid_top, gain_ref[2:3, :], summed, d_resid, gain_parts, rows, True)
+            r.d_pair[k, :, far_lanes] = r.cross_taken[k]
+        drain.allow(0)
+        square_grads(rows, CROSS, [(r.turned, r.d_pair.at[0]), (r.turned, r.d_pair.at[1])], nothing)
+        drain.begin(CROSS)
+        project_back(r.d_pair.at[0], r.square.at[FIRST], r.summed, rows, True)
+        drain.tick(CROSS, 0)
+        project_back(r.d_pair.at[1], r.square.at[SECOND], r.summed, rows, False)
+        drain.tick(CROSS, 1)
+        normalize_back(r.resid_top, r.gains[2:3, :], r.summed, r.d_resid, r.gain_parts, rows, True)
         gain_done(2)
-        turn(third, rows)
-        square_grad(rows, d_pair.at[0], FIRST)
-        square_grad(rows, d_pair.at[1], SECOND)
-        to_bf16(d_resid, d_branch, rows)
-        feed_back(rows, None)
-        normalize_back(resid_mid, gain_ref[1:2, :], summed, d_resid, gain_parts, rows, False)
+        drain.tick(CROSS, 2)
+        to_bf16(r.d_resid, r.d_branch, rows)
+        turn(r.d_branch, r.turned, rows)
+        drain.tick(CROSS, 3)
+        feed_grads(rows, r.turned, 0, OUTER, nothing)
+        drain.ticks(CROSS, 4, drain.count)
+        drain.begin(OUTER)
+        drain.end(CROSS)
+        feed_back(rows, False, OUTER)
+        drain.free(1)
+        normalize_back(r.resid_mid, r.gains[1:2, :], r.summed, r.d_resid, r.gain_parts, rows, False)
         gain_done(1)
-        turn(second, rows)
-        feed_grads(rows, d_active, 6 * block)
-        turn(d_branch, rows)
-        feed_grads(rows, active, 6 * block + inner.shape[2])
+        turn(r.second, r.turned, rows)
+        drain.allow(1)
+        feed_grads(rows, r.turned, tensor, INNER, nothing)
+        drain.ticks(OUTER, tensor, drain.count)
+        drain.begin(INNER)
+        drain.end(OUTER)
         for copy in trades + mixtures + returns + answers:
             copy.wait_send()
-        self_backward(span, rows, first_row, mirror)
-        to_bf16(d_resid, rows_out, rows)
+
+        def send_rows():
+            to_bf16(r.d_resid, r.rows_out, rows)
+            drain.home()
+
+        self_backward(span, rows, first_row, INNER, send_rows)
 
     @pl.when(here.pipe == 1)
     def _():
@@ -919,96 +983,124 @@
         first_row = pl.multiple_of(c * rows, rows)
         key_at = lax.broadcasted_iota(jnp.int32, (span, rows), 0)
         query_at = lax.broadcasted_iota(jnp.int32, (span, rows), 1) + first_row
-        same = segments(dec_row, (span, 1), 0, 0) == segments(dec_row, (1, rows), 1, first_row)
-        mask[0:span, 0:rows] = masked(same & (query_at >= key_at))
-        untangle()
-        self_forward(span, rows, first_row)
-        normalize(resid_mid, gain_ref[1:2, :], third, rows)
-        project(third, square.at[FIRST], joined, rows)
+        same = segments(lengths_row(nrow), (span, 1), 0, 0) == segments(lengths_row(nrow), (1, rows), 1, first_row)
+        r.mask[0:span, 0:rows] = masked(same & (query_at >= key_at))
+        supply.ticks(ATTN, 2, 4)
+        first_block = c * (tensor // 2)
+        rows_ready(span, rows, first_block)
+        for k in range(rows // places):
+            r.d_branch[k * places : (k + 1) * places, :] = r.x[1, first_block + k]
+        supply.ticks(ATTN, 4, supply.count - 1)
+        supply.begin(CROSS)
+        supply.ticks(ATTN, supply.count - 1, supply.count)
+        supply.finish(ATTN)
+        self_forward(span, rows, first_row, CROSS, INNER)
+        untangle(r.raw_c, FIRST, 2)
+        normalize(r.resid_mid, r.gains[1:2, :], r.third, rows)
+        project(r.third, r.square.at[FIRST], r.joined, rows)
         asks = []
         for k in range(CORES):
-            send_pair[k, 0:rows, :] = joined[:, k * half_width : (k + 1) * half_width]
-            asks.append(move(send_pair.at[k, pl.ds(0, rows)], parted(cross_queries, c, rows), 2 + k, 2 + c, across[k]))
+            r.send_pair[k, 0:rows, :] = r.joined[:, lane_halves[k]]
+            asks.append(move(r.send_pair.at[k, pl.ds(0, rows)], part_here(r.cross_queries), 2 + k, 2 + c, across[k]))
             asks[-1].start()
-        wait_loads()
-        cotangent = pl.ds(pl.multiple_of(span + first_row, rows), rows)
-        d_branch[0:rows, :] = x_ref[cotangent, :]
+        supply.ticks(INNER, 0, supply.count - 1)
+        supply.begin(OUTER)
+        supply.ticks(INNER, supply.count - 1, supply.count)
+        supply.finish(INNER)
+        supply.ticks(OUTER, 0, supply.count)
+        supply.finish(OUTER)
 
         @pl.loop(0, tensor)
         def _(tt):
-            def body(at):
-                slope[tt, rows : 2 * rows, at] = nn(d_branch[0:rows, :], outer[tt, :, at])
-
-            columns_of(inner.shape[2], body)
-
+            def body(at, k):
+                r.ff[tensor + tt, rows : 2 * rows, at] = nn(r.d_branch[0:rows, :], r.outer[tt, :, at]).astype(BF16)
+
+            columns_of(units, body)
+
+        supply.close()
+        drain.free(0)
+        r.resid_top[0:rows, :] = r.resid_mid[0:rows, :]
         for k in range(CORES):
-            move(cross_in.at[k], cross_in.at[k], 4 + k, 4 + k, across[k]).wait_recv()
-            joined[:, k * half_width : (k + 1) * half_width] = cross_in[k]
-        resid_top[0:rows, :] = resid_mid[0:rows, :]
-        project_back(joined, square.at[SECOND], resid_top, rows, False)
-        normalize(resid_top, gain_ref[2:3, :], second, rows)
-        feed_forward(rows)
-        feed_back(rows, slope)
-        d_resid[0:rows, :] = d_branch[0:rows, :].astype(F32)
-        normalize_back(resid_top, gain_ref[2:3, :], summed, d_resid, gain_parts, rows, False)
+            move(r.cross_in.at[k], r.cross_in.at[k], 4 + k, 4 + k, across[k]).wait_recv()
+            r.joined[:, lane_halves[k]] = r.cross_in[k]
+        project_back(r.joined, r.square.at[SECOND], r.resid_top, rows, False)
+        normalize(r.resid_top, r.gains[2:3, :], r.second, rows)
+        feed_forward(rows, None)
+        feed_back(rows, True, None)
+        r.d_resid[0:rows, :] = r.d_branch[0:rows, :].astype(F32)
+        normalize_back(r.resid_top, r.gains[2:3, :], r.summed, r.d_resid, r.gain_parts, rows, False)
         gain_done(2)
-        to_bf16(d_resid, branch, rows)
-        project(branch, square.at[SECOND], d_queries, rows)
+        to_bf16(r.d_resid, r.branch, rows)
+        project(r.branch, r.square.at[SECOND], r.d_pair.at[0], rows)
         tells = []
         for k in range(CORES):
-            send_back[k] = d_queries[0:rows, k * half_width : (k + 1) * half_width]
-            tells.append(move(send_back.at[k], parted(cross_back, c, rows), 6 + k, 6 + c, across[k]))
+            r.send_back[k] = r.d_pair[0, 0:rows, lane_halves[k]]
+            tells.append(move(r.send_back.at[k], part_here(r.cross_back), 6 + k, 6 + c, across[k]))
             tells[-1].start()
-        feed_out(resid_top, rows)
-        to_bf16(resid_top, rows_out, rows)
-        turn(second, rows)
-        feed_grads(rows, d_active, 6 * block)
-        turn(d_branch, rows)
-        feed_grads(rows, active, 6 * block + inner.shape[2])
-        turn(branch, rows)
-        square_grad(rows, joined, SECOND)
+        feed_out(r.resid_top, rows, None)
+        drain.free(1)
+        to_bf16(r.resid_top, r.rows_out, rows)
+        turn(r.d_branch, r.turned, rows)
+        drain.allow(0)
+        feed_grads(rows, r.turned, 0, OUTER, nothing)
+        drain.begin(OUTER)
+        turn(r.second, r.turned, rows)
+        drain.allow(1)
+        feed_grads(rows, r.turned, tensor, INNER, lambda tt, k: drain.tick(OUTER, tt, k == 0))
+        turn(r.branch, r.turned, rows)
+        turn(r.third, r.turned_more, rows)
+        drain.ticks(OUTER, tensor, drain.count)
+        drain.begin(INNER)
+        drain.end(OUTER)
         for k in range(CORES):
-            move(cross_in_back.at[k], cross_in_back.at[k], 8 + k, 8 + k, across[k]).wait_recv()
-            joined[:, k * half_width : (k + 1) * half_width] = cross_in_back[k]
-        project_back(joined, square.at[FIRST], summed, rows, True)
-        normalize_back(resid_mid, gain_ref[1:2, :], summed, d_resid, gain_parts, rows, False)
+            move(r.cross_in_back.at[k], r.cross_in_back.at[k], 8 + k, 8 + k, across[k]).wait_recv()
+            r.d_pair[1, 0:rows, lane_halves[k]] = r.cross_in_back[k]
+        project_back(r.d_pair.at[1], r.square.at[FIRST], r.summed, rows, True)
+        drain.tick(INNER, 0)
+        normalize_back(r.resid_mid, r.gains[1:2, :], r.summed, r.d_resid, r.gain_parts, rows, False)
         gain_done(1)
-        turn(third, rows)
-        square_grad(rows, joined, FIRST)
+        drain.tick(INNER, 1)
+        square_grads(
+            rows, CROSS, [(r.turned_more, r.d_pair.at[1]), (r.turned, r.joined)], lambda k: drain.tick(INNER, 2 + k)
+        )
+        drain.ticks(INNER, 2 + tensor // 2, drain.count)
+        drain.begin(CROSS)
+        drain.end(INNER)
         for copy in asks + tells:
             copy.wait_send()
-        self_backward(span, rows, first_row, mirror)
-        to_bf16(d_resid, rows_out.at[pl.ds(rows, rows)], rows)
-
-
-def parted(array, c, rows):
-    return array.at[pl.ds(pl.multiple_of(c * rows, rows), rows)]
-
-
-def blocks(tensor, dp, heads_at, rows, weights, gains, lengths, tables, buckets):
-    tall, width = rows.shape
+
+        def send_rows():
+            to_bf16(r.d_resid, r.rows_out.at[pl.ds(rows, rows)], rows)
+            drain.home()
+
+        self_backward(span, rows, first_row, CROSS, send_rows)
+
+    drain.close()
+
+
+def held(*shape, dtype=BF16):
+    return pltpu.VMEM(shape, dtype)
+
+
+def arrays(tensor, heads_at, places, width, units, ranges, kinds):
+    tall = 2 * tensor * places
     block = width // tensor
-    hidden_block = (weights.shape[2] - 6 * block) // 2
     half_rows, half_width = tall // 2, width // 2
     heads = heads_at * tensor
-    ranges = buckets.shape[1]
-    sems = pltpu.SemaphoreType.DMA
-
-    def held(*shape, dtype=BF16):
-        return pltpu.VMEM(shape, dtype)
-
-    scratch = dict(
-        raw=held(tensor, width, 6 * block),
+    return dict(
+        x=held(2, tensor, places, width),
+        own_x=held(half_rows, width),
+        raw_a=held(tensor, width, 4 * block),
+        raw_c=held(tensor, width, 2 * block),
         square=held(6, width, width),
-        inner=held(tensor, width, hidden_block),
-        outer=held(tensor, width, hidden_block),
+        inner=held(tensor, width, units),
+        outer=held(tensor, width, units),
         hidden=held(tall, width),
         keys=held(tall, width),
         values=held(tall, width),
         queries=held(half_rows, width),
         probs=held(heads, tall, half_rows),
         mask=held(tall, half_rows, dtype=F32),
-        cross_mask=held(tall, half_rows, dtype=F32),
         mixture=held(half_rows, width),
         resid_mid=held(half_rows, width, dtype=F32),
         resid_top=held(half_rows, width, dtype=F32),
@@ -1016,9 +1108,7 @@
         summed=held(half_rows, width, dtype=F32),
         second=held(half_rows, width),
         third=held(half_rows, width),
-        slope=held(tensor, half_rows, hidden_block, dtype=F32),
-        active=held(tensor, half_rows, hidden_block),
-        d_active=held(tensor, half_rows, hidden_block),
+        ff=held(2 * tensor, half_rows, units),
         d_branch=held(half_rows, width),
         branch=held(half_rows, width),
         cross_keys=held(tall, half_width),
@@ -1029,43 +1119,681 @@
         cross_back=held(half_rows, half_width),
         cross_in=held(CORES, half_rows // 2, half_width),
         cross_in_back=held(CORES, half_rows // 2, half_width),
-        d_cross_keys=held(tall, half_width),
-        d_cross_values=held(tall, half_width),
-        d_cross_queries=held(half_rows, half_width),
         cross_taken=held(CORES, half_rows, half_width),
         send_pair=held(CORES, half_rows, half_width),
         send_back=held(CORES, half_rows // 2, half_width),
         joined=held(half_rows // 2, width),
-        d_keys=held(tall, width),
-        d_values=held(tall, width),
-        d_queries=held(half_rows, width),
         taken_pair=held(2, half_rows, width),
         d_pair=held(2, half_rows, width),
         turned=held(width, half_rows),
-        stage=held(2, width, hidden_block),
+        turned_more=held(width, half_rows),
+        stage=held(2, width, units),
         vectors=held(8 * tensor, ranges, dtype=F32),
         diagonals=held(8 * tensor, ranges, dtype=F32),
-        onehot=held(LANES, ranges, dtype=F32),
+        onehot=held(kinds, ranges, dtype=F32),
         gain_parts=held(8, width, dtype=F32),
-        load_sem=sems((3, tensor)),
-        stage_sem=sems((2,)),
-        send_sem=sems((14,)),
-        recv_sem=sems((14,)),
+        send_sem=pltpu.SemaphoreType.DMA((14,)),
+        recv_sem=pltpu.SemaphoreType.DMA((14,)),
     )
+
+
+def group_columns(block, units):
+    return {ATTN: (0, 4 * block), CROSS: (4 * block, 2 * block), INNER: (6 * block, units), OUTER: (6 * block + units, units)}
+
+
+def landing(r):
+    return {ATTN: r.raw_a, CROSS: r.raw_c, INNER: r.inner, OUTER: r.outer}
+
+
+class Loads:
+    count = 7
+
+    def __init__(self, r, tensor, x_hbm, w_hbm, sems):
+        columns = group_columns(r.raw_a.shape[2] // 4, r.inner.shape[2])
+        self.x = pltpu.make_async_copy(x_hbm, r.x, sems.at[4, 0])
+        self.weights = [
+            [
+                pltpu.make_async_copy(w_hbm.at[tt, :, pl.ds(*columns[group])], target.at[tt], sems.at[group, tt])
+                for tt in range(tensor)
+            ]
+            for group, target in landing(r).items()
+        ]
+
+    def start(self):
+        self.x.start()
+        for group in self.weights:
+            for copy in group:
+                copy.start()
+
+    def rows(self):
+        self.x.wait()
+
+    def finish(self, group):
+        for copy in self.weights[group]:
+            copy.wait()
+
+    small = begin = tick = ticks = close = nothing
+
+
+class Stores:
+    count = 5
+
+    def __init__(self, r, grads_hbm, sems):
+        self.columns = group_columns(r.raw_a.shape[2] // 4, r.inner.shape[2])
+        self.r, self.grads, self.sems = r, grads_hbm, sems
+
+    def copy(self, group, tt, slot):
+        first, wide = self.columns[group]
+        return pltpu.make_async_copy(
+            self.r.stage.at[slot, :, pl.ds(0, wide)], self.grads.at[tt, :, pl.ds(first, wide)], self.sems.at[slot]
+        )
+
+    def emit(self, group, tt, slot):
+        self.copy(group, tt, slot).start()
+
+    def release(self, group, tt, slot):
+        self.copy(group, tt, slot).wait()
+
+    free = allow = begin = tick = ticks = end = home = small_begin = close = nothing
+
+
+def blocks_kernel(tensor, dp, heads_at, names, *refs):
+    here = Place(tensor, dp)
+    r = types.SimpleNamespace(**dict(zip(names, refs)))
+    across = [{"pipe": 1 - here.pipe, "dp": here.group * CORES + k} for k in range(CORES)]
+    meet([here.sibling()] + across)
+    work(r, here, Loads(r, tensor, r.x_hbm, r.w_hbm, r.load_sem), Stores(r, r.grads_hbm, r.stage_sem), tensor, heads_at)
+
+
+def blocks(tensor, dp, heads_at, kinds, rows, weights, gains, lengths, tables, buckets):
+    places, width = rows.shape[2:]
+    units = (weights.shape[2] - 6 * (width // tensor)) // 2
+    half_rows = tensor * places
+    scratch = arrays(tensor, heads_at, places, width, units, buckets.shape[1], kinds)
+    scratch["load_sem"] = pltpu.SemaphoreType.DMA((5, tensor))
+    scratch["stage_sem"] = pltpu.SemaphoreType.DMA((2,))
+    names = ["x_hbm", "w_hbm", "gains", "lengths", "tables", "buckets", "grads_hbm", "rows_out", "gains_out", "bias_out"]
     return pl.pallas_call(
-        functools.partial(block_kernel, tensor, dp, heads_at),
+        functools.partial(blocks_kernel, tensor, dp, heads_at, names + list(scratch)),
         out_shape=(
             jax.ShapeDtypeStruct(weights.shape, BF16),
             jax.ShapeDtypeStruct((half_rows, width), BF16),
             jax.ShapeDtypeStruct((8, width), F32),
             jax.ShapeDtypeStruct((8 * tensor, LANES), F32),
         ),
-        in_specs=[VMEM, ANY] + [VMEM] * 4,
+        in_specs=[ANY, ANY] + [VMEM] * 4,
         out_specs=(ANY, VMEM, VMEM, VMEM),
         scratch_shapes=list(scratch.values()),
         compiler_params=pltpu.CompilerParams(collective_id=2, has_side_effects=True, vmem_limit_bytes=VMEM_LIMIT),
         name="blocks",
     )(rows, weights, gains, lengths, tables, buckets)
+
+
+class Rings:
+    def __init__(self, r, here, tensor, dp):
+        self.r, self.here, self.tensor, self.dp = r, here, tensor, dp
+        self.depth = r.value_w.shape[0]
+        self.hops = here.chips // 2
+        self.count = 2 * self.hops - 1
+        self.sibling = here.sibling()
+        self.targets = [here.neighbour(1), here.neighbour(-1)]
+        self.landing = landing(r)
+
+
+    def block_out(self, i):
+        r, t, c = self.r, self.here.t, self.here.core
+        return pltpu.make_async_remote_copy(
+            r.rows.at[i], r.x.at[:, t], r.block_send.at[i], r.block_recv.at[t],
+            device_id={"tensor": r.rows.shape[0] * c + i}, device_id_type=MESH,
+        )
+
+    def block_kept(self, i):
+        return pltpu.make_async_copy(self.r.rows.at[i], self.r.x.at[:, self.here.t], self.r.local_sem.at[0])
+
+    def block_pass(self, source, s):
+        r = self.r
+        return pltpu.make_async_remote_copy(
+            source, r.x.at[:, s], r.pass_send.at[s], r.pass_recv.at[s], device_id=self.sibling, device_id_type=MESH
+        )
+
+    def blocks(self, mine, others):
+        for i in range(self.r.rows.shape[0]):
+            here = self.r.rows.shape[0] * self.here.core + i == self.here.t
+
+            @pl.when(here)
+            def _():
+                mine(i)
+
+            @pl.when(jnp.logical_not(here))
+            def _():
+                others(i)
+
+    def small_copies(self):
+        r, t = self.r, self.here.t
+        copies = [
+            pltpu.make_async_remote_copy(
+                r.lengths_in, r.lengths.at[self.here.core], r.small_send.at[0], r.small_recv.at[0],
+                device_id=self.sibling, device_id_type=MESH,
+            ),
+            pltpu.make_async_copy(r.lengths_in, r.lengths.at[self.here.core], r.local_sem.at[1]),
+            pltpu.make_async_copy(r.table_in, r.tables.at[t], r.local_sem.at[2]),
+        ]
+        for k in range(1, self.tensor):
+            copies.append(
+                pltpu.make_async_remote_copy(
+                    r.table_in, r.tables.at[t], r.small_send.at[k], r.small_recv.at[k],
+                    device_id={"tensor": lax.rem(t + k, self.tensor)}, device_id_type=MESH,
+                )
+            )
+        return copies
+
+
+    def slot(self, group, ring, sub):
+        line, at = self.here.at(ring)
+        half = self.depth // 2
+        first = pl.multiple_of((line * CORES + self.here.core) * self.depth + half * sub, 16)
+        return self.landing[group].at[at, pl.ds(first, half), :]
+
+    def packed(self, group, sub):
+        half = self.depth // 2
+        wide = self.landing[group].shape[2]
+        return self.r.stage.at[0, pl.ds(group * self.depth + half * sub, half), pl.ds(0, wide)]
+
+    def copies(self, group, step, part, sub, first=False):
+        r, here = self.r, self.here
+        way = -1 if part else 1
+        slot = self.slot(group, lax.rem(here.ring - way * step + here.chips, here.chips), sub)
+        source = self.packed(group, sub) if first else slot
+        onward = lambda: pltpu.make_async_remote_copy(
+            source, slot, r.ring_send.at[group, part, sub, step], r.ring_recv.at[group, part, sub, step],
+            device_id=self.targets[part], device_id_type=MESH,
+        )
+        over = lambda: pltpu.make_async_remote_copy(
+            source, slot, r.core_send.at[group, part, sub, step], r.core_recv.at[group, part, sub, step],
+            device_id=self.sibling, device_id_type=MESH,
+        )
+        return onward, over
+
+    def own(self, group):
+        wide = self.landing[group].shape[2]
+        first = pl.multiple_of(self.here.d * self.depth, 16)
+        return pltpu.make_async_copy(
+            self.r.stage.at[0, pl.ds(group * self.depth, self.depth), pl.ds(0, wide)],
+            self.landing[group].at[self.here.t, pl.ds(first, self.depth), :],
+            self.r.own_sem.at[group],
+        )
+
+    def begin(self, group):
+        for sub in range(2):
+            for part in range(2):
+                onward, over = self.copies(group, 0, part, sub, True)
+                onward().start()
+                if part == 0:
+                    over().start()
+        self.own(group).start()
+
+    def tick(self, group, n):
+        last = lax.div(n, self.count - 1)
+        step = lax.div(n, 2) + 1
+        for part in range(2):
+            sub = lax.rem(n, 2) + last * part
+            self.copies(group, step - 1, part, sub)[0]().wait_recv()
+            onward, over = self.copies(group, step, part, sub)
+            goes = jnp.logical_or(step < self.hops - 1, jnp.logical_and(step == self.hops - 1, sub == part))
+
+            @pl.when(goes)
+            def _():
+                onward().start()
+
+            over().start()
+
+    def ticks(self, group, first, last):
+        if first < last:
+
+            @pl.loop(first, last)
+            def _(n):
+                self.tick(group, n)
+
+    def finish(self, group):
+        self.each_over(group, lambda copy: copy.wait_recv())
+        self.own(group).wait()
+
+    def each_over(self, group, do):
+        for sub in range(2):
+            do(self.copies(group, 0, 0, sub)[1]())
+            do(self.copies(group, self.hops, sub, sub)[1]())
+
+        @pl.loop(1, self.hops)
+        def _(step):
+            for part in range(2):
+                for sub in range(2):
+                    do(self.copies(group, step, part, sub)[1]())
+
+    def start(self):
+        r, depth = self.r, self.depth
+        self.blocks(
+            lambda i: (self.block_kept(i).start(), self.block_pass(r.rows.at[i], self.here.t).start()),
+            lambda i: self.block_out(i).start(),
+        )
+        block = r.value_w.shape[1]
+
+        def band(group, pieces):
+            wide = pieces[0].shape[1]
+            for k, piece in enumerate(pieces):
+                r.stage[0, group * depth : (group + 1) * depth, k * wide : (k + 1) * wide] = piece
+
+        band(ATTN, [r.query_key_w[1], r.value_w[...], r.query_key_w[0], r.out_w[...].T])
+        self.begin(ATTN)
+        for copy in self.small_copies():
+            copy.start()
+        band(INNER, [r.inner_w[...]])
+        band(OUTER, [r.outer_w[...].T])
+        band(CROSS, [r.first_w[...], r.second_w[...]])
+
+    def small(self):
+        for copy in self.small_copies():
+            copy.wait()
+
+    def rows(self):
+        r, t = self.r, self.here.t
+        takes = lax.div(t, r.rows.shape[0]) == self.here.core
+        for s in range(self.tensor):
+
+            @pl.when(jnp.logical_and(takes, s != t))
+            def _():
+                pltpu.make_async_remote_copy(
+                    r.rows.at[0], r.x.at[:, s], r.block_send.at[0], r.block_recv.at[s],
+                    device_id=self.sibling, device_id_type=MESH,
+                ).wait_recv()
+                self.block_pass(r.x.at[:, s], s).start()
+
+        self.blocks(lambda i: self.block_kept(i).wait(), nothing)
+        for s in range(self.tensor):
+
+            @pl.when(jnp.logical_not(takes))
+            def _():
+                self.block_pass(r.x.at[:, s], s).wait_recv()
+
+    def close(self):
+        r, t = self.r, self.here.t
+        takes = lax.div(t, r.rows.shape[0]) == self.here.core
+        self.blocks(
+            lambda i: self.block_pass(r.rows.at[i], t).wait_send(),
+            lambda i: self.block_out(i).wait_send(),
+        )
+        for s in range(self.tensor):
+
+            @pl.when(jnp.logical_and(takes, s != t))
+            def _():
+                self.block_pass(r.x.at[:, s], s).wait_send()
+
+        for group in (ATTN, CROSS, INNER, OUTER):
+            self.each_over(group, lambda copy: copy.wait_send())
+
+            @pl.loop(0, self.hops - 1)
+            def _(step):
+                for part in range(2):
+                    for sub in range(2):
+                        self.copies(group, step, part, sub)[0]().wait_send()
+
+            for part in range(2):
+                self.copies(group, self.hops - 1, part, part)[0]().wait_send()
+
+
+class Sums:
+    def __init__(self, r, here, tensor, dp):
+        self.r, self.here, self.tensor, self.dp = r, here, tensor, dp
+        self.depth = r.value_w.shape[0]
+        self.hops = here.chips // 2
+        self.count = 2 * self.hops - 3
+        self.sibling = here.sibling()
+        self.targets = [here.neighbour(1), here.neighbour(-1)]
+        self.box = {CROSS: r.raw_c, OUTER: r.raw_a, INNER: r.inner, ATTN: r.outer}
+        self.kept = {CROSS: r.own_cross, OUTER: r.own_outer, INNER: r.own_inner, ATTN: r.ff}
+
+    def free(self, k):
+        for device in self.targets + [self.sibling]:
+            pl.semaphore_signal(self.r.free_sem.at[k], inc=1, device_id=device, device_id_type=MESH)
+
+    def allow(self, k):
+        pl.semaphore_wait(self.r.free_sem.at[k], 3)
+
+    def boxed(self, group, index, first, height):
+        at = pl.ds(pl.multiple_of(lax.rem(index, self.dp) * self.depth + first, 16), height)
+        return (lax.div(index, self.dp), at, slice(None))
+
+    def taken(self, group, step, part, first, height):
+        index = 0 if isinstance(step, int) and step == 0 else step + part * (self.hops - 1) * jnp.minimum(step, 1)
+        return self.boxed(group, index, first, height)
+
+    def theirs(self, group, ring, first, height):
+        return self.boxed(group, self.here.chips - 1 + ring, first, height)
+
+    def own(self, group, ring, first, height):
+        return (ring, pl.ds(first, height), slice(None))
+
+    def ring_of(self, line, at):
+        return line * self.tensor + at + (line % 2) * (self.tensor - 1 - 2 * at)
+
+    def pieces(self, group, tt, slot):
+        r, depth = self.r, self.depth
+        wide = self.box[group].shape[2]
+        made = []
+        for line in range(self.here.groups):
+            ring = self.ring_of(line, tt)
+
+            def rows_of(core):
+                return r.stage.at[slot, pl.ds(pl.multiple_of((line * CORES + core) * depth, 16), depth), pl.ds(0, wide)]
+
+            made.append(
+                pltpu.make_async_copy(
+                    rows_of(self.here.core), self.kept[group].at[self.own(group, ring, 0, depth)], r.kept_sem.at[group, ring]
+                )
+            )
+            made.append(
+                pltpu.make_async_remote_copy(
+                    rows_of(1 - self.here.core), self.box[group].at[self.theirs(group, ring, 0, depth)],
+                    r.pair_send.at[group, ring], r.pair_recv.at[group, ring], device_id=self.sibling, device_id_type=MESH,
+                )
+            )
+        return made
+
+    def emit(self, group, tt, slot):
+        for piece in self.pieces(group, tt, slot):
+            piece.start()
+
+    def release(self, group, tt, slot):
+        for k, piece in enumerate(self.pieces(group, tt, slot)):
+            if k % 2:
+                piece.wait_send()
+            else:
+                piece.wait()
+
+
+    def rows_at(self, sub):
+        half = self.depth // 2
+        return pl.multiple_of(half * sub, 16), half
+
+    def source(self, step, part):
+        way = -1 if part else 1
+        return lax.rem(self.here.ring + way * (self.hops - step) + self.here.chips, self.here.chips)
+
+    def onward(self, group, step, part, sub):
+        r = self.r
+        first, height = self.rows_at(sub)
+        return pltpu.make_async_remote_copy(
+            self.kept[group].at[self.own(group, self.source(step, part), first, height)],
+            self.box[group].at[self.taken(group, step, part, first, height)],
+            r.sum_send.at[group, part, sub, step], r.sum_recv.at[group, part, sub, step],
+            device_id=self.targets[part], device_id_type=MESH,
+        )
+
+    def here_sum(self, group, ring, first, height):
+        value = self.kept[group][self.own(group, ring, first, height)].astype(F32)
+        return value + self.box[group][self.theirs(group, ring, first, height)].astype(F32)
+
+    def advance(self, group, step, part, sub, fresh=False):
+        if not fresh:
+            self.onward(group, step - 1, part, sub).wait_recv()
+        first, height = self.rows_at(sub)
+        value = self.here_sum(group, self.source(step, part), first, height)
+        if not fresh:
+            value = value + self.box[group][self.taken(group, step - 1, part, first, height)].astype(F32)
+        self.kept[group][self.own(group, self.source(step, part), first, height)] = value.astype(BF16)
+        self.onward(group, step, part, sub).start()
+
+    def begin(self, group):
+        @pl.loop(0, self.here.chips)
+        def _(ring):
+            pltpu.make_async_remote_copy(
+                self.kept[group].at[self.own(group, ring, 0, self.depth)],
+                self.box[group].at[self.theirs(group, ring, 0, self.depth)],
+                self.r.pair_send.at[group, ring], self.r.pair_recv.at[group, ring], device_id=self.sibling, device_id_type=MESH,
+            ).wait_recv()
+
+        for part in range(2):
+            self.advance(group, 0, part, part, True)
+        for part in range(2):
+            self.advance(group, 1, part, 1 - part, True)
+        if group == ATTN:
+            self.small_across().wait_recv()
+            self.small_advance(0, 0, True)
+            self.small_advance(1, 1, True)
+
+    def tick(self, group, n, when=True):
+        step, leads = lax.div(n + 1, 2) + 1, lax.rem(n, 2)
+
+        @pl.when(when)
+        def _():
+            for part in range(2):
+                self.advance(group, step, part, (1 - part) * leads + part * (1 - leads))
+            if group == ATTN:
+
+                @pl.when(leads == 0)
+                def _():
+                    self.small_advance(step, 0)
+
+                    @pl.when(step > 1)
+                    def _():
+                        self.small_advance(step, 1)
+
+    def ticks(self, group, first, last):
+        if first < last:
+
+            @pl.loop(first, last)
+            def _(n):
+                self.tick(group, n)
+
+    def end(self, group):
+        r, last = self.r, self.hops - 1
+        for sub in range(2):
+            first, height = self.rows_at(sub)
+            value = self.here_sum(group, self.here.ring, first, height)
+            for part in range(2):
+                self.onward(group, last, part, sub).wait_recv()
+                value = value + self.box[group][self.taken(group, last, part, first, height)].astype(F32)
+            target = r.inner_out if group == INNER else r.total
+            target[pl.ds(first, height), 0 : self.box[group].shape[2]] = value
+        block = r.value_w.shape[1]
+        if group == ATTN:
+            r.pair_out[1] = r.total[:, 0:block]
+            r.value_out[...] = r.total[:, block : 2 * block]
+            r.pair_out[0] = r.total[:, 2 * block : 3 * block]
+            r.out_out[...] = r.total[:, 3 * block : 4 * block].T
+            at = self.small_at(self.here.ring)
+            value = r.small[at] + r.small_theirs[at]
+            for part in range(2):
+                self.small_onward(last, part).wait_recv()
+                value = value + r.small_taken[part, last]
+            r.tiny_out[...] = value
+        if group == CROSS:
+            r.first_out[...] = r.total[:, 0:block]
+            r.second_out[...] = r.total[:, block : 2 * block]
+        if group == OUTER:
+            r.outer_out[...] = r.total[...].T
+
+
+    def small_at(self, ring):
+        line, at = self.here.at(ring)
+        return at, line * CORES + self.here.core
+
+    def small_across(self):
+        r = self.r
+        return pltpu.make_async_remote_copy(
+            r.small, r.small_theirs, r.small_sem.at[0], r.small_sem.at[1], device_id=self.sibling, device_id_type=MESH
+        )
+
+    def small_onward(self, step, part):
+        r = self.r
+        return pltpu.make_async_remote_copy(
+            r.small_sent.at[part, step], r.small_taken.at[part, step], r.tiny_send.at[part, step], r.tiny_recv.at[part, step],
+            device_id=self.targets[part], device_id_type=MESH,
+        )
+
+    def small_advance(self, step, part, fresh=False):
+        at = self.small_at(self.source(step, part))
+        value = self.r.small[at] + self.r.small_theirs[at]
+        if not fresh:
+            self.small_onward(step - 1, part).wait_recv()
+            value = value + self.r.small_taken[part, step - 1]
+        self.r.small_sent[part, step] = value
+        self.small_onward(step, part).start()
+
+    def small_begin(self):
+        r, depth = self.r, self.depth
+        r.small[...] = jnp.zeros_like(r.small)
+        kinds = r.onehot.shape[0] // self.dp
+        heads_at = self.heads_at
+        for tt in range(self.tensor):
+            for d in range(self.dp):
+                r.small[tt, d, 0:3, 0:depth] = r.gains_out[0:3, d * depth : (d + 1) * depth]
+                r.small[tt, d, 3 : 3 + heads_at, 0:kinds] = r.bias_out[
+                    8 * tt : 8 * tt + heads_at, d * kinds : (d + 1) * kinds
+                ]
+        self.small_across().start()
+
+
+    def home_copy(self, k):
+        r, here, tensor = self.r, self.here, self.tensor
+        nrow, half, places = r.home_in.shape[0], tensor // 2, r.home_in.shape[2]
+        place = here.pipe * (here.core * half + k % half) + (1 - here.pipe) * k
+        which = here.pipe * (k // half) + (1 - here.pipe) * here.core
+        owner = lax.div(here.t, nrow)
+        source = r.rows_out.at[pl.ds(k * places, places)]
+        slot = r.home_in.at[lax.rem(here.t, nrow), which]
+        recv = r.home_recv.at[lax.rem(here.t, nrow), which]
+        return (
+            jnp.logical_and(place == here.t, owner == here.core),
+            lambda: pltpu.make_async_copy(source, slot, recv),
+            lambda: pltpu.make_async_remote_copy(
+                source, slot, r.home_send.at[k], recv,
+                device_id={"dp": here.group * CORES + owner, "tensor": place}, device_id_type=MESH,
+            ),
+        )
+
+    def home(self):
+        for k in range(self.tensor):
+            stays, inside, away = self.home_copy(k)
+
+            @pl.when(stays)
+            def _():
+                inside().start()
+
+            @pl.when(jnp.logical_not(stays))
+            def _():
+                away().start()
+
+    def close(self):
+        r = self.r
+        places = r.home_in.shape[2]
+        for i in range(r.home_in.shape[0]):
+            for which in range(2):
+                pltpu.make_async_copy(
+                    r.rows_out.at[pl.ds(0, places)], r.home_in.at[i, which], r.home_recv.at[i, which]
+                ).wait()
+                r.home_out[i, which] = r.home_in[i, which].astype(F32)
+        for k in range(self.tensor):
+            stays, inside, away = self.home_copy(k)
+
+            @pl.when(jnp.logical_not(stays))
+            def _():
+                away().wait_send()
+
+        self.small_across().wait_send()
+
+        for part in range(2):
+            self.small_onward(0 + part, part).wait_send()
+            for group in (ATTN, CROSS, INNER, OUTER):
+                self.onward(group, 0, part, part).wait_send()
+                self.onward(group, 1, part, 1 - part).wait_send()
+                self.onward(group, 1, part, part).wait_send()
+        self.small_onward(1, 0).wait_send()
+
+        @pl.loop(2, self.hops)
+        def _(step):
+            for part in range(2):
+                self.small_onward(step, part).wait_send()
+                for group in (ATTN, CROSS, INNER, OUTER):
+                    for sub in range(2):
+                        self.onward(group, step, part, sub).wait_send()
+
+
+def fits_fused(tensor, dp, depth, units, width):
+    chips = tensor * dp // CORES
+    return (
+        depth % 32 == 0
+        and 4 * depth <= width
+        and chips <= 2 * tensor
+        and chips == 2 * tensor == 8
+        and units == width == 6 * LANES
+    )
+
+
+def fused_kernel(tensor, dp, heads_at, names, *refs):
+    here = Place(tensor, dp)
+    r = types.SimpleNamespace(**dict(zip(names, refs)))
+    line = [
+        {"dp": here.group * CORES + lax.rem(here.core + j, CORES), "tensor": lax.rem(here.t + k, tensor)}
+        for j in range(CORES)
+        for k in range(tensor)
+        if j + k > 0
+    ]
+    across = [{"pipe": 1 - here.pipe, "dp": here.group * CORES + k} for k in range(CORES)]
+    meet([here.neighbour(1), here.neighbour(-1)] + line + across)
+    supply, drain = Rings(r, here, tensor, dp), Sums(r, here, tensor, dp)
+    drain.heads_at = heads_at
+    work(r, here, supply, drain, tensor, heads_at)
+
+
+def fused(tensor, dp, heads_at, kinds, rows, lengths, table, gains, buckets, weights):
+    nrow, two, places, width = rows.shape
+    depth, block = weights[1].shape
+    units = weights[5].shape[1]
+    chips = tensor * dp // CORES
+    wide = -(-max(depth, kinds // dp) // LANES) * LANES
+    sems = pltpu.SemaphoreType.DMA
+    scratch = arrays(tensor, heads_at, places, width, units, buckets.shape[1], kinds)
+    scratch.update(
+        lengths=pltpu.VMEM((CORES,) + lengths.shape, lengths.dtype),
+        tables=pltpu.VMEM((tensor,) + table.shape, table.dtype),
+        own_cross=held(chips, depth, 2 * block),
+        own_outer=held(chips, depth, units),
+        own_inner=held(chips, depth, units),
+        total=held(depth, units, dtype=F32),
+        rows_out=held(tensor * places, width),
+        gains_out=held(8, width, dtype=F32),
+        bias_out=held(8 * tensor, LANES, dtype=F32),
+        home_in=held(nrow, two, places, width),
+        small=held(tensor, dp, 8, wide, dtype=F32),
+        small_theirs=held(tensor, dp, 8, wide, dtype=F32),
+        small_sent=held(2, chips // 2, 8, wide, dtype=F32),
+        small_taken=held(2, chips // 2, 8, wide, dtype=F32),
+        block_send=sems((nrow,)), block_recv=sems((tensor,)), pass_send=sems((tensor,)), pass_recv=sems((tensor,)),
+        local_sem=sems((3,)), small_send=sems((tensor,)), small_recv=sems((tensor,)), own_sem=sems((4,)),
+        ring_send=sems((4, 2, 2, chips)), ring_recv=sems((4, 2, 2, chips)),
+        core_send=sems((4, 2, 2, chips)), core_recv=sems((4, 2, 2, chips)),
+        kept_sem=sems((4, chips)), pair_send=sems((4, chips)), pair_recv=sems((4, chips)),
+        sum_send=sems((4, 2, 2, chips)), sum_recv=sems((4, 2, 2, chips)),
+        small_sem=sems((2,)), tiny_send=sems((2, chips // 2)), tiny_recv=sems((2, chips // 2)),
+        home_send=sems((tensor,)), home_recv=sems((nrow, two)),
+        free_sem=pltpu.SemaphoreType.REGULAR((2,)),
+    )
+    inputs = ["rows", "lengths_in", "table_in", "gains", "buckets"]
+    inputs += ["query_key_w", "value_w", "out_w", "first_w", "second_w", "inner_w", "outer_w"]
+    outputs = dict(
+        home_out=rows.shape, tiny_out=(8, wide), pair_out=(2, depth, block), value_out=(depth, block),
+        out_out=(block, depth), first_out=(depth, block), second_out=(depth, block), inner_out=(depth, units),
+        outer_out=(units, depth),
+    )
+    return pl.pallas_call(
+        functools.partial(fused_kernel, tensor, dp, heads_at, inputs + list(outputs) + list(scratch)),
+        out_shape=tuple(jax.ShapeDtypeStruct(shape, F32) for shape in outputs.values()),
+        in_specs=[ANY] + [VMEM] * 11,
+        out_specs=(VMEM,) * len(outputs),
+        scratch_shapes=list(scratch.values()),
+        compiler_params=pltpu.CompilerParams(collective_id=3, has_side_effects=True, vmem_limit_bytes=VMEM_LIMIT),
+        name="fused",
+    )(rows, lengths, table, gains, buckets, *weights)
 
 
 def pad_to(array, *shape):
@@ -1078,47 +1806,56 @@
 ):
     nrow = section_rows.shape[1]
     depth, block = value_w.shape[1:]
-    buckets, heads_at = rel_bias.shape[1:]
+    kinds, heads_at = rel_bias.shape[1:]
     on_encoder = lax.axis_index("pipe") == 0
-    pack = jnp.concatenate(
-        [query_key_w[0, 1], value_w[0], query_key_w[0, 0], attn_out_w[0].T, cross_first[0], cross_second[0], ff_in[0], ff_out[0].T],
-        axis=1,
-    )
     lengths = pad_to(jnp.concatenate([enc_lengths, dec_lengths], axis=0), 8, LANES)
     table = pad_to(rel_bias[0].T, 8, LANES)
-    rows, weights, lengths, tables = gather(tensor, dp, section_rows[0], pack, lengths, table)
     ranges = -(-enc_buckets.shape[0] // LANES) * LANES
     dec_all = jnp.concatenate([jnp.zeros((dec_buckets.shape[0] - 1,), jnp.int32), dec_buckets])
     bucket_row = jnp.where(on_encoder, pad_to(enc_buckets, ranges), pad_to(dec_all, ranges))
+    bucket_rows = jnp.broadcast_to(bucket_row[None], (8, ranges))
     width = section_rows.shape[-1]
-    grads, finished, gains, bias = blocks(
-        tensor, dp, heads_at, rows.reshape(-1, width), weights.reshape(tensor, width, -1),
-        pad_to(norm_gains[0], 8, width), lengths, tables, jnp.broadcast_to(bucket_row[None], (8, ranges)),
+    gains = pad_to(norm_gains[0], 8, width)
+    held_kinds = kinds // dp
+    weights = (query_key_w[0], value_w[0], attn_out_w[0], cross_first[0], cross_second[0], ff_in[0], ff_out[0])
+    if fits_fused(tensor, dp, depth, ff_in.shape[2], width):
+        home, tiny, pair, value, out, first, second, inner, outer = fused(
+            tensor, dp, heads_at, kinds, section_rows[0], lengths, table, gains, bucket_rows, weights
+        )
+        grads = (pair, value, out, first, second, inner, outer)
+    else:
+        home, tiny, grads = in_three(
+            tensor, dp, heads_at, kinds, section_rows[0], lengths, table, gains, bucket_rows, weights
+        )
+    return (
+        home.astype(F32)[None],
+        tiny[:3, :depth][None],
+        tiny[3 : 3 + heads_at, :held_kinds].T[None],
+    ) + tuple(grad[None] for grad in grads)
+
+
+def in_three(tensor, dp, heads_at, kinds, section_rows, lengths, table, gains, buckets, weights):
+    query_key, value, out, first, second, inner, outer = weights
+    nrow, _, _, width = section_rows.shape
+    depth, block = value.shape
+    units = inner.shape[1]
+    pack = jnp.concatenate([query_key[1], value, query_key[0], out.T, first, second, inner, outer.T], axis=1)
+    rows, gathered, lengths, tables = gather(tensor, dp, section_rows, pack, lengths, table)
+    grads, finished, gain_grads, bias = blocks(
+        tensor, dp, heads_at, kinds, rows, gathered.reshape(tensor, width, -1), gains, lengths, tables, buckets
     )
-    held = buckets // dp
-    wide = -(-max(depth, held) // LANES) * LANES
-    gain_part = pad_to(gains[:3].reshape(3, dp, depth).transpose(1, 0, 2), dp, 3, wide)
-    bias_part = bias.reshape(tensor, 8, LANES)[:, :heads_at, :buckets].reshape(tensor, heads_at, dp, held)
+    held_kinds = kinds // dp
+    wide = -(-max(depth, held_kinds) // LANES) * LANES
+    gain_part = pad_to(gain_grads[:3].reshape(3, dp, depth).transpose(1, 0, 2), dp, 3, wide)
+    bias_part = bias.reshape(tensor, 8, LANES)[:, :heads_at, :kinds].reshape(tensor, heads_at, dp, held_kinds)
     bias_part = pad_to(bias_part.transpose(0, 2, 1, 3), tensor, dp, 5, wide)
     small = jnp.concatenate([jnp.broadcast_to(gain_part[None], (tensor,) + gain_part.shape), bias_part], axis=2)
     total, tiny, home = scatter(
         tensor, dp, grads.reshape(tensor, dp, depth, -1), small, finished.reshape(tensor, -1, width), nrow
     )
-    names = ("key", "value", "query", "out", "first", "second")
-    part = {name: total[:, k * block : (k + 1) * block] for k, name in enumerate(names)}
-    hidden_block = ff_in.shape[2]
-    return (
-        home.astype(F32)[None],
-        tiny[:3, :depth][None],
-        tiny[3 : 3 + heads_at, :held].T[None],
-        jnp.stack([part["query"], part["key"]])[None],
-        part["value"][None],
-        part["out"].T[None],
-        part["first"][None],
-        part["second"][None],
-        total[:, 6 * block : 6 * block + hidden_block][None],
-        total[:, 6 * block + hidden_block :].T[None],
-    )
+    key, value, query, out, first, second = [total[:, k * block : (k + 1) * block] for k in range(6)]
+    inner, outer = total[:, 6 * block : 6 * block + units], total[:, 6 * block + units :]
+    return home, tiny, (jnp.stack([query, key]), value, out.T, first, second, inner, outer.T)
 
 
 def solution(mesh):

time: 331 us -> 272 us (0.82)
  Pallas kernels: 305 us -> 254 us
  other arithmetic: 4.87 us -> 0.08 us
    pallas_call x3 -> x1, Pallas kernels: 305 us -> 254 us  [fused(): pl.pallas_call(functools.partial(fused_kernel, tensor, dp, heads_at, inpu...]
    unnamed x8 -> x39, local copies, waits for them, and re-layouts: 4.32 us -> 12.6 us
    broadcast_in_dim x5 -> x2, local copies, waits for them, and re-layouts: 4.86 us -> 1.29 us  [the longest x1 0.67 us: shards(): tiny[3:3 + heads_at, :held_kinds].T[None]]
where the time goes in v2:
time: 272 us; the launch traced here: 271 us
  Pallas kernels  254 us (93%)
  local copies, waits for them, and re-layouts  16.5 us (6%)
    pallas_call x1, Pallas kernels, fused(): pl.pallas_call(functools.partial(fused_kernel, tensor, dp, heads_at, inpu...  254 us
    unnamed x39, local copies, waits for them, and re-layouts  12.6 us

profile of v2, /device:TPU:8, one launch (start us, length us, event | category | flops | bytes accessed | tf_op | source)
XLA Modules:
  0.0 271.5 jit_solution(4756474896107227071)
XLA Ops:
  0.6 1.9 copy.24
  2.5 0.7 copy-done.8
  3.2 0.0 copy-done.10
  3.2 0.1 pad_select_fusion
  3.3 0.6 broadcast_in_dim.37.refs_4_
  3.9 0.1 copy-done.7
  4.0 0.6 pad.23.refs_3_
  4.6 0.1 copy-done.11
  4.7 0.0 copy-done.12
  4.7 0.6 pad.21.refs_1_
  5.3 0.1 copy-done.9
  5.4 0.6 pad.22.refs_2_
  6.0 254.2 %fused.1 = (f32[2,2,64,768]{3,2,1,0:T(8,128)}, f32[8,256]{1,0:T(8,128)}, f32[2,192,192]{2,1,0:T(8,128)}, f32[192,192]{1,0:T(8,128)}, f32[192,192]{1,0:T(8,128)},...) custom-call(bf16[2,2,64,768]{3,2,1,0:T(8,128)(2,1)} %bitcast.35, ...), custom_call_target="tpu_custom_call" | custom-call | tf_op jit(solution)/shard_map/fused/pallas_call | solution.py:1788
  260.2 0.0 copy-start
  260.2 0.8 slice_bitcast_fusion
  261.0 0.6 copy.25
  261.5 0.7 slice_bitcast_fusion.1
  262.2 0.6 copy.26
  262.8 2.2 copy.27
  265.0 0.0 copy-done
  265.0 0.9 copy.41
  265.9 0.4 copy-done.2
  266.2 0.7 copy.42
  267.0 0.3 copy-done.6
  267.3 0.7 copy.43
  268.0 0.3 copy-done.5
  268.3 0.7 copy.44
  269.0 0.7 copy.45
  269.7 0.3 copy-done.3
  270.0 0.7 copy.46
  270.6 0.0 copy-done.1
  270.6 0.8 copy.47
  (16 shorter events, 0.0 us)
Async XLA Ops:
  2.5 0.7 copy-start.8
  2.5 0.7 copy-start.10
  3.3 0.7 copy-start.7
  4.0 0.7 copy-start.11
  4.0 0.7 copy-start.12
  4.7 0.7 copy-start.9
  260.2 4.8 %copy-start = (f32[2,2,64,768]{3,2,1,0:T(8,128)S(1)}, f32[2,2,64,768]{3,2,1,0:T(8,128)}, u32[]{:S(2)}) copy-start(f32[2,2,64,768]{3,2,1,0:T(8,128)} %get-tuple-element.19) | copy-start | bytes 2359300
  265.0 1.2 copy-start.2
  266.2 1.1 copy-start.6
  267.3 1.0 copy-start.5
  267.3 1.7 copy-start.4
  268.3 2.4 copy-start.1
  269.0 1.0 copy-start.3
